TPU v7x, 512 devices: a whole 4x4x16 slice. The times are simulated.
512 devices in a mesh: prow: 16 (over x, z_hi), pcol: 32 (over z_lo, y, core).
Axes of the slice: x: 4, y: 4, z: 16 (z_hi: 4, z_lo: 4; z = z_hi * 4 + z_lo), core: 2. Of those that a mesh axis runs over, the one named last changes fastest.
Arguments:
- panel: float32 [4096, 4096], P('pcol', 'prow'), may hold values from -1.2 to 1.2
- ancestor_inverse: float32 [4096, 4096], P('prow', 'pcol'), as said below
- diag_inverse: float32 [4096, 2048], P(('prow', 'pcol')), may hold values from -6 to 6
- pattern: int32 [32, 32], replicated, may hold values from 0 to 1, as said below
Outputs:
- inverse_rows: float32 [4096, 4096], P('prow', 'pcol')
- diag_blocks: float32 [4096, 2048], P(('prow', 'pcol'))
Inputs may be any that keep to these rules, and one draw needn't show every extreme that they name: pattern[i, j] is 1 where block (i, j) of 128 x 128 entries of the panel is structurally nonzero, else 0. ancestor_inverse is symmetric.
All inputs are finite; a program needn't handle non-finite values.
Results may differ from a plain program's by a relative error of at most 0.0001.
Values sent between devices are 32-bit elements; how exact they have to be, the bound alone decides.
No kernel may reach another device: no remote copies, remote signals or barrier semaphores. Data moves between devices by JAX's collectives and lax.ppermute only.
A program may use at most 64 MiB of HBM per device.

v0:
```python
import jax
import jax.numpy as jnp
from jax import lax
from jax.sharding import PartitionSpec as P

BLOCK = 128


highest = lax.Precision.HIGHEST


def from_root(array, axis, root):
    mine = lax.axis_index(axis) == root
    return lax.psum(jnp.where(mine, array, jnp.zeros_like(array)), axis)


def block_mask(pattern, row_begin, row_total, col_begin, col_total):
    block_rows, block_cols = pattern.shape
    row_ids = (row_begin + lax.iota(jnp.int32, row_total)) // BLOCK
    col_ids = (col_begin + lax.iota(jnp.int32, col_total)) // BLOCK
    row_onehot = (row_ids[:, None] == lax.iota(jnp.int32, block_rows)[None, :]).astype(jnp.float32)
    col_onehot = (col_ids[:, None] == lax.iota(jnp.int32, block_cols)[None, :]).astype(jnp.float32)
    pattern_float = pattern.astype(jnp.float32)
    picked = jnp.dot(
        row_onehot, pattern_float, precision=highest, preferred_element_type=jnp.float32
    )
    return lax.dot_general(
        picked,
        col_onehot,
        (((1,), (1,)), ((), ())),
        precision=highest,
        preferred_element_type=jnp.float32,
    )


def on_device(panel, ancestor_inverse, diag_inverse, pattern):
    prow_size = lax.axis_size("prow")
    pcol_size = lax.axis_size("pcol")
    row_index = lax.axis_index("prow")
    col_index = lax.axis_index("pcol")
    local_rows, local_cols = panel.shape
    masked = panel * block_mask(
        pattern, col_index * local_rows, local_rows, row_index * local_cols, local_cols
    )
    gathered = lax.all_gather(masked, "pcol", axis=0, tiled=True)
    share_cols = ancestor_inverse.shape[1]
    column_ratio = pcol_size // prow_size
    offset = col_index % column_ratio * share_cols
    owner_piece = lax.dynamic_slice_in_dim(gathered, offset, share_cols, 1)
    owner_row = col_index // column_ratio
    total_rows = gathered.shape[0]
    own_count = total_rows // prow_size
    own_start = row_index * own_count
    sibling_width = diag_inverse.shape[1]
    sibling_start = own_start // sibling_width * sibling_width
    relayed = from_root(owner_piece, "prow", owner_row)
    sibling_panel = lax.dynamic_slice_in_dim(relayed, sibling_start, sibling_width, 0)
    partial_rows = -jnp.dot(
        gathered, ancestor_inverse, precision=highest, preferred_element_type=jnp.float32
    )
    summed = lax.psum(partial_rows, "prow")
    inverse_rows = lax.dynamic_slice_in_dim(summed, own_start, own_count, 0)
    coupling = lax.psum_scatter(
        lax.dot_general(
            inverse_rows,
            sibling_panel,
            (((1,), (1,)), ((), ())),
            precision=highest,
            preferred_element_type=jnp.float32,
        ),
        "pcol",
        scatter_dimension=0,
        tiled=True,
    )
    return (inverse_rows, diag_inverse - coupling)


def solution(mesh):
    return jax.shard_map(
        on_device,
        mesh=mesh,
        in_specs=(P("pcol", "prow"), P("prow", "pcol"), P(("prow", "pcol"), None), P()),
        out_specs=(P("prow", "pcol"), P(("prow", "pcol"), None)),
        check_vma=False,
    )
```

profile of v0, /device:TPU:1, one launch (start us, length us, event | category | flops | bytes accessed | tf_op | source)
XLA Modules:
  0.0 659.7 jit_solution(11327499613395002623)
XLA Ops:
  7.2 0.0 copy-start
  7.2 0.0 all-gather.2.cloned.1.call-start
  7.3 0.9 fusion.3
  8.2 1.9 convolution_multiply_fusion
  10.1 0.0 all-gather.2.cloned.1.call-update
  10.1 0.0 all-reduce.3.cloned.1.call-start
  10.2 74.3 %all-gather.2.cloned.1.call-done = f32[4096,256]{1,0:T(8,128)} async-done(((f32[128,256]{1,0:T(8,128)}), f32[4096,256]{1,0:T(8,128)}) %all-gather.2.cloned.1.call-update) | async-done | bytes 4194320 | tf_op jit(solution)/shard_map/all_gather | solution.py:45
  84.5 0.0 copy-done
  84.5 0.0 copy-start.1
  84.5 7.1 %convolution_negate_fusion = f32[4096,128]{1,0:T(8,128)} fusion(f32[4096,256]{1,0:T(8,128)} %all-gather.2.cloned.1.call-done, f32[256,128]{1,0:T(8,128)S(1)} %copy-done), kind=kOutput, calls=%fused_computation | convolution fusion | flops 1611137024 | bytes 6422528 | tf_op jit(solution)/shard_map/dot_general | solution.py:58
  91.6 0.0 copy-done.1
  91.6 1.5 dynamic-slice_select_fusion
  93.1 0.0 all-reduce.3.cloned.1.call-update
  93.1 0.0 reduce-scatter.2.cloned.1.call-start
  93.2 406.5 %all-reduce.3.cloned.1.call-done = (f32[4096,128]{1,0:T(8,128)}, f32[4096,128]{1,0:T(8,128)}) async-done(((f32[4096,128]{1,0:T(8,128)}, f32[4096,128]{1,0:T(8,128)}), (f32[4096,128]{1,0:T(8,128)}, f32[4096,128]{1,0:T(8,128)})) %all-reduce.3.cloned.1.call-update) | async-done | bytes 4194320 | tf_op jit(solution)/shard_map/psum | solution.py:61
  499.7 0.9 constant_dynamic-slice_fusion
  500.6 0.0 copy-start.2
  500.6 0.0 copy-start.3
  500.6 4.4 fusion
  505.0 0.0 reduce-scatter.2.cloned.1.call-update
  505.1 0.0 copy-done.2
  505.1 146.6 %reduce-scatter.2.cloned.1.call-done = f32[8,2048]{1,0:T(8,128)} async-done(((f32[256,2048]{1,0:T(8,128)}), f32[8,2048]{1,0:T(8,128)}) %reduce-scatter.2.cloned.1.call-update) | async-done | bytes 65552 | tf_op jit(solution)/shard_map/reduce_scatter | solution.py:63
  651.7 0.0 copy-done.3
  651.7 1.5 sub.26
  (2 shorter events, 0.0 us)
Async XLA Ops:
  7.2 77.4 %copy-start = (f32[256,128]{1,0:T(8,128)S(1)}, f32[256,128]{1,0:T(8,128)}, u32[]{:S(2)}) copy-start(f32[256,128]{1,0:T(8,128)} %param.5) | copy-start | bytes 393220
  7.2 77.4 %all-gather.2.cloned.1.call-start = ((), (), s32[]{:S(2)}) async-start(), calls=%async_computation.1 | async-start | bytes 4325376 | tf_op jit(solution)/shard_map/all_gather | solution.py:45
  10.1 489.6 %all-reduce.3.cloned.1.call-start = ((), (), s32[]{:S(2)}) async-start(), calls=%async_computation.3 | async-start | bytes 8388608 | tf_op jit(solution)/shard_map/psum | solution.py:61
  84.5 7.1 %copy-start.1 = (f32[4096,256]{1,0:T(8,128)S(1)}, f32[4096,256]{1,0:T(8,128)}, u32[]{:S(2)}) copy-start(f32[4096,256]{1,0:T(8,128)} %all-gather.2.cloned.1.call-done) | copy-start | bytes 12582916
  93.1 558.5 %reduce-scatter.2.cloned.1.call-start = ((), (), s32[]{:S(2)}) async-start(), calls=%async_computation.2 | async-start | bytes 2162688 | tf_op jit(solution)/shard_map/reduce_scatter | solution.py:63
  500.6 4.5 copy-start.2
  500.6 151.0 %copy-start.3 = (f32[8,2048]{1,0:T(8,128)S(1)}, f32[8,2048]{1,0:T(8,128)}, u32[]{:S(2)}) copy-start(f32[8,2048]{1,0:T(8,128)} %param.6) | copy-start | bytes 196612
Sparse Core Ops, SparseCore 0:
  10.7 73.7 all-gather.1
  93.3 406.3 all-reduce.2
  505.2 146.4 reduce-scatter.1
where the time goes:
time: 664 us; the launch traced here: 660 us
  waiting for transfers between devices  627 us (94%)
  matrix products  14.3 us (2%)
  between operations  13.9 us (2%)
    psum x1, waiting for transfers between devices, on_device(): summed = lax.psum(partial_rows, 'prow')  406 us
    reduce_scatter x1, waiting for transfers between devices, on_device(): lax.psum_scatter(lax.dot_general(inverse_rows, sibling_panel, (((1,), (1,...  147 us
    all_gather x1, waiting for transfers between devices, on_device(): gathered = lax.all_gather(masked, 'pcol', axis=0, tiled=True)  74.3 us
  transfers between devices with their start and end apart: 3, of which 3 were waited for; matrix products, arithmetic and copies ran while one was open for 0% of the time, Pallas kernels for 0%

commit v1 on v0

v1 whole, which is shorter than its diff:
```python
import jax
import jax.numpy as jnp
from jax import lax
from jax.sharding import Mesh, PartitionSpec as P

AXES = ("x", "zh", "zl", "y", "c")
SIZES = (4, 4, 4, 4, 2)
high = lax.Precision.HIGH


def flat(x, zh, zl, y, c):
    return (((x * 4 + zh) * 4 + zl) * 4 + y) * 2 + c


def everyone():
    return [
        (x, zh, zl, y, c)
        for x in range(4)
        for zh in range(4)
        for zl in range(4)
        for y in range(4)
        for c in range(2)
    ]


def shift_pairs(step):
    return [(i, (i + step) % 4) for i in range(4)]


def column_form_pairs(step):
    return [
        (flat(x, zh, zl, y, c), flat(zl, (y + step) % 4, x, zh, c))
        for x, zh, zl, y, c in everyone()
    ]


def pick(blocks, index):
    return lax.dynamic_index_in_dim(blocks, index, 0, keepdims=False)


def on_device(panel, ancestor_inverse, diag_inverse, pattern):
    x = lax.axis_index("x")
    zh = lax.axis_index("zh")
    zl = lax.axis_index("zl")
    y = lax.axis_index("y")
    c = lax.axis_index("c")

    own = lax.dynamic_slice(
        pattern, ((zl * 4 + y) * 2 + c, (x * 4 + zh) * 2), (1, 2)
    ).astype(jnp.float32)
    masked = panel * jnp.repeat(own, 128, axis=1)

    a_cols = lax.all_gather(ancestor_inverse, "c", axis=1, tiled=True)

    over_zl = lax.all_gather(masked, "zl", axis=0, tiled=True)

    col_blocks = [
        lax.ppermute(masked, AXES, column_form_pairs(t)) for t in range(4)
    ]

    by_y = [over_zl] + [
        lax.ppermute(over_zl, "y", shift_pairs(s)) for s in (1, 2, 3)
    ]
    gathered = jnp.stack([g.reshape(4, 128, 256) for g in by_y], axis=1)
    partial = jnp.dot(
        gathered.reshape(2048, 256), a_cols, precision=high,
        preferred_element_type=jnp.float32,
    )
    over_x = lax.all_to_all(partial, "x", 0, 0, tiled=True)
    sum_x = jnp.sum(over_x.reshape(4, 4, 128, 256), axis=0)
    ordered = jnp.stack([pick(sum_x, (y - b) % 4) for b in range(4)])
    over_zh = lax.all_to_all(ordered, "zh", 0, 0, tiled=True)
    half_rows = -jnp.sum(over_zh, axis=0)
    rows = lax.all_gather(half_rows, "c", axis=0, tiled=True)
    inverse_rows = lax.dynamic_slice_in_dim(rows, c * 128, 128, 1)

    col_half = jnp.concatenate(col_blocks, axis=0)
    col_other = lax.ppermute(col_half, "x", [(i, i ^ 1) for i in range(4)])
    col_form = jnp.concatenate([col_half, col_other], axis=0)

    lhs = rows.reshape(4, 4, 16, 256).transpose(1, 0, 2, 3).reshape(256, 256)
    coupling = lax.dot_general(
        lhs, col_form, (((1,), (1,)), ((), ())), precision=high,
        preferred_element_type=jnp.float32,
    )
    over_y = lax.all_to_all(coupling, "y", 0, 0, tiled=True)
    sum_y = jnp.sum(over_y.reshape(4, 64, 1024), axis=0)
    over_l = lax.all_to_all(sum_y, "zl", 0, 0, tiled=True)
    sum_l = jnp.sum(over_l.reshape(4, 16, 1024), axis=0)
    both = lax.all_to_all(sum_l, "c", 0, 0, tiled=True).reshape(2, 8, 2, 4, 128)
    blocks = both.transpose(2, 3, 1, 0, 4)
    blocks = jnp.stack([pick(blocks, (b + x) % 2) for b in range(2)])
    blocks = jnp.stack(
        [
            lax.dynamic_index_in_dim(blocks, (zh - b) % 4, 1, keepdims=False)
            for b in range(4)
        ],
        axis=1,
    )
    total = blocks.transpose(2, 0, 1, 3, 4).reshape(8, 2048)
    return (inverse_rows, diag_inverse - total)


def solution(mesh):
    fine = Mesh(mesh.devices.reshape(SIZES), AXES)
    prow, pcol = ("x", "zh"), ("zl", "y", "c")
    return jax.shard_map(
        on_device,
        mesh=fine,
        in_specs=(P(pcol, prow), P(prow, pcol), P(AXES, None), P()),
        out_specs=(P(prow, pcol), P(AXES, None)),
        check_vma=False,
    )
```

time: 664 us -> 217 us (0.33)
  waiting for transfers between devices: 627 us -> 53.1 us
  starting transfers between devices: 0.12 us -> 102 us
  blocking collectives: 0 us -> 52.4 us
  between operations: 13.9 us -> 0.86 us
  matrix products: 14.3 us -> 2.97 us
    psum x1 -> x0, waiting for transfers between devices: 406 us -> none  [on_device(): summed = lax.psum(partial_rows, 'prow')]
    reduce_scatter x1 -> x0, waiting for transfers between devices: 147 us -> none  [on_device(): lax.psum_scatter(lax.dot_general(inverse_rows, sibling_panel, (((1,), (1,...]
    all_gather x1 -> x0, waiting for transfers between devices: 74.3 us -> none  [on_device(): gathered = lax.all_gather(masked, 'pcol', axis=0, tiled=True)]
    ppermute x0 -> x8, starting transfers between devices: none -> 74 us  [the longest x1 32.5 us: on_device(): col_other = lax.ppermute(col_half, 'x', [(i, i ^ 1) for i in range(4)])]
    all_to_all x0 -> x3, waiting for transfers between devices: none -> 29.5 us  [the longest x1 24.5 us: on_device(): over_x = lax.all_to_all(partial, 'x', 0, 0, tiled=True)]
    all_to_all x0 -> x3, starting transfers between devices: none -> 28 us  [the longest x1 10.9 us: on_device(): over_l = lax.all_to_all(sum_y, 'zl', 0, 0, tiled=True)]
    all_gather x0 -> x3, blocking collectives: none -> 27.4 us  [the longest x1 16.3 us: on_device(): over_zl = lax.all_gather(masked, 'zl', axis=0, tiled=True)]
    all_to_all x0 -> x2, blocking collectives: none -> 25.1 us  [the longest x1 17.3 us: on_device(): over_y = lax.all_to_all(coupling, 'y', 0, 0, tiled=True)]
  transfers between devices with their start and end apart: 3 -> 11, of which waited for: 3 -> 7; matrix products, arithmetic and copies ran while one was open for 0% -> 0% of each run, Pallas kernels for 0% -> 0%
where the time goes in v1:
time: 217 us
  starting transfers between devices  102 us (47%)
  waiting for transfers between devices  53.1 us (24%)
  blocking collectives  52.4 us (24%)
  other arithmetic  4.39 us (2%)
  matrix products  2.97 us (1%)
    ppermute x1, starting transfers between devices, on_device(): col_other = lax.ppermute(col_half, 'x', [(i, i ^ 1) for i in range(4)])  32.5 us
    ppermute x4, starting transfers between devices, on_device(): lax.ppermute(masked, AXES, column_form_pairs(t))  30.8 us
    all_to_all x1, waiting for transfers between devices, on_device(): over_x = lax.all_to_all(partial, 'x', 0, 0, tiled=True)  24.5 us
    all_to_all x1, blocking collectives, on_device(): over_y = lax.all_to_all(coupling, 'y', 0, 0, tiled=True)  17.3 us
    all_gather x1, blocking collectives, on_device(): over_zl = lax.all_gather(masked, 'zl', axis=0, tiled=True)  16.3 us
    all_to_all x1, starting transfers between devices, on_device(): over_l = lax.all_to_all(sum_y, 'zl', 0, 0, tiled=True)  10.9 us
    all_to_all x1, starting transfers between devices, on_device(): over_zh = lax.all_to_all(ordered, 'zh', 0, 0, tiled=True)  10.8 us
    ppermute x3, starting transfers between devices, on_device(): lax.ppermute(over_zl, 'y', shift_pairs(s))  10.7 us
  transfers between devices with their start and end apart: 11, of which 7 were waited for; matrix products, arithmetic and copies ran while one was open for 0% of the time, Pallas kernels for 0%

profile of v1, /device:TPU:1, one launch (start us, length us, event | category | flops | bytes accessed | tf_op | source)
XLA Modules:
  0.0 216.7 jit_solution(8881922176474055173)
XLA Ops:
  0.6 0.8 convert_bitcast_fusion
  1.5 0.9 broadcast_multiply_fusion
  2.4 16.3 %all_gather.9 = f32[512,256]{1,0:T(8,128)S(1)} all-gather(f32[128,256]{1,0:T(8,128)S(1)} %broadcast_multiply_fusion), channel_id=1, replica_groups=mesh['x'=4,'zh'=4,'zl'=4,'y'=4,'c'=2] {'zl'}, dimensions={0}, use_global_device_ids=true | all-gather | bytes 655360 | tf_op jit(solution)/shard_map/all_gather | solution.py:55
  18.7 3.2 %collective-permute-start = (f32[512,256]{1,0:T(8,128)S(1)}, f32[512,256]{1,0:T(8,128)S(1)}, u32[]{:S(2)}, u32[]{:S(2)}) collective-permute-start(f32[512,256]{1,0:T(8,128)S(1)} %all_gather.9), channel_id=1, source_target_pairs={{0,2},{2,4},{4,6},{6,0},{1,3},{3,5},{5,7},{7,1},{8,10},{10,12},{12... | collective-permute-start | bytes 1572872 | tf_op jit(solution)/shard_map/ppermute | solution.py:62
  21.9 4.5 %collective-permute-start.1 = (f32[512,256]{1,0:T(8,128)S(1)}, f32[512,256]{1,0:T(8,128)S(1)}, u32[]{:S(2)}, u32[]{:S(2)}) collective-permute-start(f32[512,256]{1,0:T(8,128)S(1)} %all_gather.9), channel_id=1, source_target_pairs={{0,4},{2,6},{4,0},{6,2},{1,5},{3,7},{5,1},{7,3},{8,12},{10,14},{12... | collective-permute-start | bytes 1572872 | tf_op jit(solution)/shard_map/ppermute | solution.py:62
  26.5 3.0 %collective-permute-start.2 = (f32[512,256]{1,0:T(8,128)S(1)}, f32[512,256]{1,0:T(8,128)S(1)}, u32[]{:S(2)}, u32[]{:S(2)}) collective-permute-start(f32[512,256]{1,0:T(8,128)S(1)} %all_gather.9), channel_id=1, source_target_pairs={{0,6},{2,0},{4,2},{6,4},{1,7},{3,1},{5,3},{7,5},{8,14},{10,8},{12,... | collective-permute-start | bytes 1572872 | tf_op jit(solution)/shard_map/ppermute | solution.py:62
  29.4 6.6 %all_gather.10 = f32[256,256]{1,0:T(8,128)S(1)} all-gather(f32[256,128]{1,0:T(8,128)} %param.5), channel_id=1, replica_groups=mesh['x'=4,'zh'=4,'zl'=4,'y'=4,'c'=2] {'c'}, dimensions={1}, use_global_device_ids=true | all-gather | bytes 393216 | tf_op jit(solution)/shard_map/all_gather | solution.py:53
  36.1 9.5 %collective-permute-done.1 = f32[512,256]{1,0:T(8,128)S(1)} collective-permute-done((f32[512,256]{1,0:T(8,128)S(1)}, f32[512,256]{1,0:T(8,128)S(1)}, u32[]{:S(2)}, u32[]{:S(2)}) %collective-permute-start.1) | collective-permute-done | bytes 524320 | tf_op jit(solution)/shard_map/ppermute | solution.py:62
  45.6 0.6 collective-permute-done.2
  46.1 0.2 pad_maximum_fusion
  46.3 2.3 %fusion.2 = f32[4,512,256]{2,1,0:T(8,128)} fusion(f32[4,512,256]{2,1,0:T(8,128)S(1)} %bitcast.40, f32[256,256]{1,0:T(8,128)S(1)} %all_gather.10), kind=kOutput, calls=%fused_computation.5 | convolution fusion | flops 805306368 | bytes 4456448 | tf_op jit(solution)/shard_map/dot_general | solution.py:65
  48.7 6.3 %all-to-all-start = ((f32[4,512,256]{2,1,0:T(8,128)}), f32[4,512,256]{2,1,0:T(8,128)S(1)}, u32[]{:S(2)}, u32[]{:S(2)}) async-start(f32[4,512,256]{2,1,0:T(8,128)} %fusion.2), calls=%async_computation | async-start | bytes 4194304 | tf_op jit(solution)/shard_map/all_to_all | solution.py:69
  55.0 24.5 %all-to-all-done = f32[4,512,256]{2,1,0:T(8,128)S(1)} async-done(((f32[4,512,256]{2,1,0:T(8,128)}), f32[4,512,256]{2,1,0:T(8,128)S(1)}, u32[]{:S(2)}, u32[]{:S(2)}) %all-to-all-start) | async-done | bytes 2097184 | tf_op jit(solution)/shard_map/all_to_all | solution.py:69
  79.5 0.2 reduce_sum.38
  79.7 0.8 pad_maximum_fusion.1
  80.6 10.8 %all-to-all-start.1 = ((f32[4,128,256]{2,1,0:T(8,128)}), f32[4,128,256]{2,1,0:T(8,128)S(1)}, u32[]{:S(2)}, u32[]{:S(2)}) async-start(f32[4,128,256]{2,1,0:T(8,128)} %pad_maximum_fusion.1), calls=%async_computation.1 | async-start | bytes 1048576 | tf_op jit(solution)/shard_map/all_to_all | solution.py:72
  91.3 0.7 collective-permute-start.3
  92.0 14.0 %collective-permute-start.4 = (f32[128,256]{1,0:T(8,128)S(1)}, f32[128,256]{1,0:T(8,128)S(1)}, u32[]{:S(2)}, u32[]{:S(2)}) collective-permute-start(f32[128,256]{1,0:T(8,128)S(1)} %broadcast_multiply_fusion), channel_id=1, source_target_pairs={{0,32},{1,33},{2,64},{3,65},{4,96},{5,97},{6,0},{7,1},{8,160},{9,1... | collective-permute-start | bytes 393224 | tf_op jit(solution)/shard_map/ppermute | solution.py:58
  106.0 13.6 %collective-permute-start.5 = (f32[128,256]{1,0:T(8,128)S(1)}, f32[128,256]{1,0:T(8,128)S(1)}, u32[]{:S(2)}, u32[]{:S(2)}) collective-permute-start(f32[128,256]{1,0:T(8,128)S(1)} %broadcast_multiply_fusion), channel_id=1, source_target_pairs={{0,64},{1,65},{2,96},{3,97},{4,0},{5,1},{6,32},{7,33},{8,192},{9,1... | collective-permute-start | bytes 393224 | tf_op jit(solution)/shard_map/ppermute | solution.py:58
  119.6 2.5 %collective-permute-start.6 = (f32[128,256]{1,0:T(8,128)S(1)}, f32[128,256]{1,0:T(8,128)S(1)}, u32[]{:S(2)}, u32[]{:S(2)}) collective-permute-start(f32[128,256]{1,0:T(8,128)S(1)} %broadcast_multiply_fusion), channel_id=1, source_target_pairs={{0,96},{1,97},{2,0},{3,1},{4,32},{5,33},{6,64},{7,65},{8,224},{9,2... | collective-permute-start | bytes 393224 | tf_op jit(solution)/shard_map/ppermute | solution.py:58
  122.3 3.4 %collective-permute-done.6 = f32[128,256]{1,0:T(8,128)S(1)} collective-permute-done((f32[128,256]{1,0:T(8,128)S(1)}, f32[128,256]{1,0:T(8,128)S(1)}, u32[]{:S(2)}, u32[]{:S(2)}) %collective-permute-start.6) | collective-permute-done | bytes 131104 | tf_op jit(solution)/shard_map/ppermute | solution.py:58
  125.7 32.5 %collective-permute-start.7 = (f32[512,256]{1,0:T(8,128)S(1)}, f32[512,256]{1,0:T(8,128)S(1)}, u32[]{:S(2)}, u32[]{:S(2)}) collective-permute-start(f32[512,256]{1,0:T(8,128)S(1)} %pad_maximum_fusion.2), channel_id=1, source_target_pairs={{0,128},{128,0},{256,384},{384,256},{1,129},{129,1},{257,385},{385... | collective-permute-start | bytes 1572872 | tf_op jit(solution)/shard_map/ppermute | solution.py:78
  158.3 10.0 %collective-permute-done.7 = f32[512,256]{1,0:T(8,128)S(1)} collective-permute-done((f32[512,256]{1,0:T(8,128)S(1)}, f32[512,256]{1,0:T(8,128)S(1)}, u32[]{:S(2)}, u32[]{:S(2)}) %collective-permute-start.7) | collective-permute-done | bytes 524320 | tf_op jit(solution)/shard_map/ppermute | solution.py:78
  168.4 4.5 %all_gather.11 = f32[256,256]{1,0:T(8,128)S(1)} all-gather(f32[128,256]{1,0:T(8,128)S(1)} %neg.3), channel_id=1, replica_groups=mesh['x'=4,'zh'=4,'zl'=4,'y'=4,'c'=2] {'c'}, dimensions={0}, use_global_device_ids=true | all-gather | bytes 393216 | tf_op jit(solution)/shard_map/all_gather | solution.py:74
  172.9 0.6 fusion
  173.5 17.3 %all_to_all.35 = f32[4,64,1024]{2,1,0:T(8,128)S(1)} all-to-all(f32[4,64,1024]{2,1,0:T(8,128)S(1)} %fusion), channel_id=1, replica_groups=mesh['x'=4,'zh'=4,'zl'=4,'y'=4,'c'=2] {'y'}, dimensions={0} | all-to-all | bytes 2097152 | tf_op jit(solution)/shard_map/all_to_all | solution.py:86
  190.8 0.8 reduce_sum.41
  191.5 10.9 %all-to-all-start.3 = ((f32[4,16,1024]{2,1,0:T(8,128)}), f32[4,16,1024]{2,1,0:T(8,128)S(1)}, u32[]{:S(2)}, u32[]{:S(2)}) async-start(f32[4,16,1024]{2,1,0:T(8,128)} %bitcast.17), calls=%async_computation.3 | async-start | bytes 524288 | tf_op jit(solution)/shard_map/all_to_all | solution.py:88
  202.5 0.7 constant_dynamic-slice_fusion
  203.1 5.0 %all-to-all-done.3 = f32[4,16,1024]{2,1,0:T(8,128)S(1)} async-done(((f32[4,16,1024]{2,1,0:T(8,128)}), f32[4,16,1024]{2,1,0:T(8,128)S(1)}, u32[]{:S(2)}, u32[]{:S(2)}) %all-to-all-start.3) | async-done | bytes 262176 | tf_op jit(solution)/shard_map/all_to_all | solution.py:88
  208.2 7.8 %all_to_all.36 = f32[2,8,1024]{2,1,0:T(8,128)S(1)} all-to-all(f32[2,8,1024]{2,1,0:T(8,128)S(1)} %bitcast.48), channel_id=1, replica_groups=mesh['x'=4,'zh'=4,'zl'=4,'y'=4,'c'=2] {'c'}, dimensions={0} | all-to-all | bytes 131072 | tf_op jit(solution)/shard_map/all_to_all | solution.py:90
  216.0 0.6 sub.27
  (23 shorter events, 0.5 us)
Async XLA Ops:
  18.7 17.4 %collective-permute-start = (f32[512,256]{1,0:T(8,128)S(1)}, f32[512,256]{1,0:T(8,128)S(1)}, u32[]{:S(2)}, u32[]{:S(2)}) collective-permute-start(f32[512,256]{1,0:T(8,128)S(1)} %all_gather.9), channel_id=1, source_target_pairs={{0,2},{2,4},{4,6},{6,0},{1,3},{3,5},{5,7},{7,1},{8,10},{10,12},{12... | collective-permute-start | bytes 1572872 | tf_op jit(solution)/shard_map/ppermute | solution.py:62
  21.9 23.7 %collective-permute-start.1 = (f32[512,256]{1,0:T(8,128)S(1)}, f32[512,256]{1,0:T(8,128)S(1)}, u32[]{:S(2)}, u32[]{:S(2)}) collective-permute-start(f32[512,256]{1,0:T(8,128)S(1)} %all_gather.9), channel_id=1, source_target_pairs={{0,4},{2,6},{4,0},{6,2},{1,5},{3,7},{5,1},{7,3},{8,12},{10,14},{12... | collective-permute-start | bytes 1572872 | tf_op jit(solution)/shard_map/ppermute | solution.py:62
  26.5 19.7 %collective-permute-start.2 = (f32[512,256]{1,0:T(8,128)S(1)}, f32[512,256]{1,0:T(8,128)S(1)}, u32[]{:S(2)}, u32[]{:S(2)}) collective-permute-start(f32[512,256]{1,0:T(8,128)S(1)} %all_gather.9), channel_id=1, source_target_pairs={{0,6},{2,0},{4,2},{6,4},{1,7},{3,1},{5,3},{7,5},{8,14},{10,8},{12,... | collective-permute-start | bytes 1572872 | tf_op jit(solution)/shard_map/ppermute | solution.py:62
  48.7 30.8 %all-to-all-start = ((f32[4,512,256]{2,1,0:T(8,128)}), f32[4,512,256]{2,1,0:T(8,128)S(1)}, u32[]{:S(2)}, u32[]{:S(2)}) async-start(f32[4,512,256]{2,1,0:T(8,128)} %fusion.2), calls=%async_computation | async-start | bytes 4194304 | tf_op jit(solution)/shard_map/all_to_all | solution.py:69
  80.6 87.7 %all-to-all-start.1 = ((f32[4,128,256]{2,1,0:T(8,128)}), f32[4,128,256]{2,1,0:T(8,128)S(1)}, u32[]{:S(2)}, u32[]{:S(2)}) async-start(f32[4,128,256]{2,1,0:T(8,128)} %pad_maximum_fusion.1), calls=%async_computation.1 | async-start | bytes 1048576 | tf_op jit(solution)/shard_map/all_to_all | solution.py:72
  91.3 30.8 %collective-permute-start.3 = (f32[128,256]{1,0:T(8,128)S(1)}, f32[128,256]{1,0:T(8,128)S(1)}, u32[]{:S(2)}, u32[]{:S(2)}) collective-permute-start(f32[128,256]{1,0:T(8,128)S(1)} %broadcast_multiply_fusion), channel_id=1, source_target_pairs={{0,0},{1,1},{2,32},{3,33},{4,64},{5,65},{6,96},{7,97},{8,128},{9,1... | collective-permute-start | bytes 393224 | tf_op jit(solution)/shard_map/ppermute | solution.py:58
  92.0 30.1 %collective-permute-start.4 = (f32[128,256]{1,0:T(8,128)S(1)}, f32[128,256]{1,0:T(8,128)S(1)}, u32[]{:S(2)}, u32[]{:S(2)}) collective-permute-start(f32[128,256]{1,0:T(8,128)S(1)} %broadcast_multiply_fusion), channel_id=1, source_target_pairs={{0,32},{1,33},{2,64},{3,65},{4,96},{5,97},{6,0},{7,1},{8,160},{9,1... | collective-permute-start | bytes 393224 | tf_op jit(solution)/shard_map/ppermute | solution.py:58
  106.0 16.3 %collective-permute-start.5 = (f32[128,256]{1,0:T(8,128)S(1)}, f32[128,256]{1,0:T(8,128)S(1)}, u32[]{:S(2)}, u32[]{:S(2)}) collective-permute-start(f32[128,256]{1,0:T(8,128)S(1)} %broadcast_multiply_fusion), channel_id=1, source_target_pairs={{0,64},{1,65},{2,96},{3,97},{4,0},{5,1},{6,32},{7,33},{8,192},{9,1... | collective-permute-start | bytes 393224 | tf_op jit(solution)/shard_map/ppermute | solution.py:58
  119.6 6.0 %collective-permute-start.6 = (f32[128,256]{1,0:T(8,128)S(1)}, f32[128,256]{1,0:T(8,128)S(1)}, u32[]{:S(2)}, u32[]{:S(2)}) collective-permute-start(f32[128,256]{1,0:T(8,128)S(1)} %broadcast_multiply_fusion), channel_id=1, source_target_pairs={{0,96},{1,97},{2,0},{3,1},{4,32},{5,33},{6,64},{7,65},{8,224},{9,2... | collective-permute-start | bytes 393224 | tf_op jit(solution)/shard_map/ppermute | solution.py:58
  125.7 42.6 %collective-permute-start.7 = (f32[512,256]{1,0:T(8,128)S(1)}, f32[512,256]{1,0:T(8,128)S(1)}, u32[]{:S(2)}, u32[]{:S(2)}) collective-permute-start(f32[512,256]{1,0:T(8,128)S(1)} %pad_maximum_fusion.2), channel_id=1, source_target_pairs={{0,128},{128,0},{256,384},{384,256},{1,129},{129,1},{257,385},{385... | collective-permute-start | bytes 1572872 | tf_op jit(solution)/shard_map/ppermute | solution.py:78
  190.8 25.2 %copy-start = (f32[8,2048]{1,0:T(8,128)S(1)}, f32[8,2048]{1,0:T(8,128)}, u32[]{:S(2)}) copy-start(f32[8,2048]{1,0:T(8,128)} %param.6) | copy-start | bytes 196612
  191.5 16.6 %all-to-all-start.3 = ((f32[4,16,1024]{2,1,0:T(8,128)}), f32[4,16,1024]{2,1,0:T(8,128)S(1)}, u32[]{:S(2)}, u32[]{:S(2)}) async-start(f32[4,16,1024]{2,1,0:T(8,128)} %bitcast.17), calls=%async_computation.3 | async-start | bytes 524288 | tf_op jit(solution)/shard_map/all_to_all | solution.py:88

commit v2 on v1

v2 whole, which is shorter than its diff:
```python
import jax
import jax.numpy as jnp
from jax import lax
from jax.sharding import Mesh, PartitionSpec as P

AXES = ("x", "zh", "zl", "y", "c")
SIZES = (4, 4, 4, 4, 2)
high = lax.Precision.HIGH


def turn_pairs():
    def flat(x, zh, zl, rest):
        return ((x * 4 + zh) * 4 + zl) * 8 + rest

    return [
        (flat(x, zh, zl, rest), flat(zl, zh, x, rest))
        for x in range(4)
        for zh in range(4)
        for zl in range(4)
        for rest in range(8)
    ]


def shift_pairs(step):
    return [(i, (i + step) % 4) for i in range(4)]


def pick(blocks, index, axis=0):
    return lax.dynamic_index_in_dim(blocks, index, axis, keepdims=False)


def dot(lhs, rhs, dims):
    return lax.dot_general(
        lhs, rhs, (dims, ((), ())), precision=high,
        preferred_element_type=jnp.float32,
    )


def on_device(panel, ancestor_inverse, diag_inverse, pattern):
    x = lax.axis_index("x")
    zh = lax.axis_index("zh")
    zl = lax.axis_index("zl")
    y = lax.axis_index("y")
    c = lax.axis_index("c")

    moved = lax.ppermute(panel, AXES, turn_pairs())
    own = lax.dynamic_slice(
        pattern, ((x * 4 + y) * 2 + c, (zl * 4 + zh) * 2), (1, 2)
    ).astype(jnp.float32)
    moved = moved * jnp.repeat(own, 128, axis=1)

    a_own = lax.all_gather(ancestor_inverse, "x", axis=0, tiled=True)
    a_other = lax.ppermute(a_own, "c", [(0, 1), (1, 0)])

    moved, a_own = lax.optimization_barrier((moved, a_own))
    over_zl = lax.all_gather(moved, "zl", axis=0)
    over_zl = over_zl.transpose(1, 0, 2).reshape(128, 1024)
    copies = lax.optimization_barrier(jnp.stack([over_zl] * 4))
    by_y = lax.all_to_all(copies, "y", 0, 0, tiled=True).reshape(512, 1024)

    moved, _ = lax.optimization_barrier((moved, copies))
    over_zh = lax.all_gather(moved, "zh", axis=0)
    by_y, over_zh = lax.optimization_barrier((by_y, over_zh))

    partial = jnp.concatenate(
        [dot(by_y, a, ((1,), (0,))) for a in (a_own, a_other)], axis=1
    )
    summed = lax.all_to_all(partial, "zh", 0, 0, tiled=True)
    summed = -jnp.sum(summed.reshape(4, 128, 256), axis=0)

    over_zh, _ = lax.optimization_barrier((over_zh, partial))
    pieces = [pick(over_zh, y)] + [
        lax.ppermute(pick(over_zh, (y + s) % 4), "y", shift_pairs(s))
        for s in (1, 2, 3)
    ]
    pieces = jnp.stack(pieces)
    col_half = jnp.concatenate([pick(pieces, (y - b) % 4) for b in range(4)])
    col_other = lax.ppermute(col_half, "x", [(i, i ^ 1) for i in range(4)])
    col_form = jnp.concatenate([col_half, col_other], axis=0)

    crossed = jnp.concatenate([summed[:, 128:], summed[:, :128]], axis=1)
    half_rows = jnp.where(c == 0, summed, crossed)
    rows = lax.all_gather(half_rows, "c", axis=0, tiled=True)
    inverse_rows = lax.dynamic_slice_in_dim(rows, c * 128, 128, 1)

    lhs = rows.reshape(4, 4, 16, 256).transpose(1, 0, 2, 3).reshape(256, 256)
    coupling = dot(lhs, col_form, ((1,), (1,)))
    over_y = lax.all_to_all(coupling, "y", 0, 0, tiled=True)
    sum_y = jnp.sum(over_y.reshape(4, 64, 1024), axis=0)
    over_l = lax.all_to_all(sum_y, ("zl", "c"), 0, 0, tiled=True)
    both = jnp.sum(over_l.reshape(4, 2, 8, 2, 4, 128), axis=0)
    both = both.transpose(2, 1, 3, 0, 4)
    both = jnp.stack([pick(both, (b + x) % 2) for b in range(2)], axis=1)
    return (inverse_rows, diag_inverse - both.reshape(8, 2048))


def solution(mesh):
    fine = Mesh(mesh.devices.reshape(SIZES), AXES)
    prow, pcol = ("x", "zh"), ("zl", "y", "c")
    return jax.shard_map(
        on_device,
        mesh=fine,
        in_specs=(P(pcol, prow), P(prow, pcol), P(AXES, None), P()),
        out_specs=(P(prow, pcol), P(AXES, None)),
        check_vma=False,
    )
```

time: 217 us -> 161 us (0.74)
  starting transfers between devices: 102 us -> 37 us
  blocking collectives: 52.4 us -> 86.3 us
  waiting for transfers between devices: 53.1 us -> 25.7 us
  local copies, waits for them, and re-layouts: 0.9 us -> 3.19 us
    all_gather x2 -> x3, blocking collectives: 22.9 us -> 65.2 us  [the longest x1 35.2 us: on_device(): over_zh = lax.all_gather(moved, 'zh', axis=0)]
    ppermute x1, starting transfers between devices: 32.5 us -> 1.92 us  [on_device(): col_other = lax.ppermute(col_half, 'x', [(i, i ^ 1) for i in range(4)])]
    ppermute x7 -> x5, starting transfers between devices: 41.5 us -> 18.3 us  [the longest x3 9.83 us: on_device(): lax.ppermute(pick(over_zh, (y + s) % 4), 'y', shift_pairs(s))]
    all_to_all x3, waiting for transfers between devices: 29.5 us -> 7.94 us  [the longest x1 7.94 us: on_device(): over_l = lax.all_to_all(sum_y, ('zl', 'c'), 0, 0, tiled=True)]
    all_to_all x3, starting transfers between devices: 28 us -> 16.8 us  [the longest x1 6.1 us: on_device(): over_l = lax.all_to_all(sum_y, ('zl', 'c'), 0, 0, tiled=True)]
    all_to_all x1 -> x0, blocking collectives: 7.79 us -> none  [on_device(): both = lax.all_to_all(sum_l, 'c', 0, 0, tiled=True).reshape(2, 8, 2, 4, 128)]
    ppermute x7 -> x5, waiting for transfers between devices: 13.5 us -> 6.11 us  [the longest x3 6.11 us: on_device(): lax.ppermute(pick(over_zh, (y + s) % 4), 'y', shift_pairs(s))]
  transfers between devices with their start and end apart: 11 -> 9, of which waited for: 7 -> 4; matrix products, arithmetic and copies ran while one was open for 0% -> 2% of each run, Pallas kernels for 0% -> 0%
where the time goes in v2:
time: 161 us; the launch traced here: 160 us
  blocking collectives  86.3 us (54%)
  starting transfers between devices  37 us (23%)
  waiting for transfers between devices  25.7 us (16%)
  matrix products  4 us (2%)
  local copies, waits for them, and re-layouts  3.19 us (2%)
  other arithmetic  3.17 us (2%)
    all_gather x1, blocking collectives, on_device(): over_zh = lax.all_gather(moved, 'zh', axis=0)  35.2 us
    all_gather x1, blocking collectives, on_device(): a_own = lax.all_gather(ancestor_inverse, 'x', axis=0, tiled=True)  17.5 us
    all_to_all x1, blocking collectives, on_device(): over_y = lax.all_to_all(coupling, 'y', 0, 0, tiled=True)  16.8 us
    all_gather x1, blocking collectives, on_device(): over_zl = lax.all_gather(moved, 'zl', axis=0)  12.5 us
    ppermute x1, waiting for transfers between devices, on_device(): col_other = lax.ppermute(col_half, 'x', [(i, i ^ 1) for i in range(4)])  11.7 us
    ppermute x3, starting transfers between devices, on_device(): lax.ppermute(pick(over_zh, (y + s) % 4), 'y', shift_pairs(s))  9.83 us
    all_to_all x1, waiting for transfers between devices, on_device(): over_l = lax.all_to_all(sum_y, ('zl', 'c'), 0, 0, tiled=True)  7.94 us
    ppermute x1, starting transfers between devices, on_device(): a_other = lax.ppermute(a_own, 'c', [(0, 1), (1, 0)])  6.9 us
  transfers between devices with their start and end apart: 9, of which 4 were waited for; matrix products, arithmetic and copies ran while one was open for 2% of the time, Pallas kernels for 0%

profile of v2, /device:TPU:1, one launch (start us, length us, event | category | flops | bytes accessed | tf_op | source)
XLA Modules:
  0.0 160.4 jit_solution(1577976655669259732)
XLA Ops:
  0.6 1.6 collective-permute-start
  2.2 0.8 convert_bitcast_fusion
  3.0 0.1 broadcast_bitcast_fusion
  3.0 17.5 %all_gather.18 = f32[1024,128]{1,0:T(8,128)S(1)} all-gather(f32[256,128]{1,0:T(8,128)} %param.5), channel_id=1, replica_groups=mesh['x'=4,'zh'=4,'zl'=4,'y'=4,'c'=2] {'x'}, dimensions={0}, use_global_device_ids=true | all-gather | bytes 655360 | tf_op jit(solution)/shard_map/all_gather | solution.py:52
  20.5 0.0 collective-permute-done
  20.5 12.5 %all-gather = f32[512,256]{1,0:T(8,128)S(1)} all-gather(f32[128,256]{1,0:T(8,128)S(1)} %broadcast_multiply_fusion), channel_id=2, replica_groups=mesh['x'=4,'zh'=4,'zl'=4,'y'=4,'c'=2] {'zl'}, dimensions={0}, use_global_device_ids=true | all-gather | bytes 655360 | tf_op jit(solution)/shard_map/all_gather | solution.py:56
  33.1 0.2 copy.33
  33.3 0.2 copy.34
  33.5 1.6 %stack.25 = f32[4,128,1024]{2,1,0:T(8,128)} broadcast(f32[128,1024]{1,0:T(8,128)S(1)} %copy.34), dimensions={1,2} | broadcast | bytes 2621440 | tf_op jit(solution)/shard_map/stack | solution.py:58
  35.1 4.7 %all-to-all-start = ((f32[4,128,1024]{2,1,0:T(8,128)}), f32[4,128,1024]{2,1,0:T(8,128)S(1)}, u32[]{:S(2)}, u32[]{:S(2)}) async-start(f32[4,128,1024]{2,1,0:T(8,128)} %stack.25), calls=%async_computation | async-start | bytes 4194304 | tf_op jit(solution)/shard_map/all_to_all | solution.py:59
  39.7 6.9 %collective-permute-start.1 = (f32[1024,128]{1,0:T(8,128)S(1)}, f32[1024,128]{1,0:T(8,128)}, u32[]{:S(2)}, u32[]{:S(2)}) collective-permute-start(f32[1024,128]{1,0:T(8,128)S(1)} %all_gather.18), channel_id=1, source_target_pairs={{0,1},{1,0},{2,3},{3,2},{4,5},{5,4},{6,7},{7,6},{8,9},{9,8},{10,11... | collective-permute-start | bytes 1572872 | tf_op jit(solution)/shard_map/ppermute | solution.py:53
  46.7 35.2 %all-gather.1 = f32[512,256]{1,0:T(8,128)S(1)} all-gather(f32[128,256]{1,0:T(8,128)S(1)} %broadcast_multiply_fusion), channel_id=3, replica_groups=mesh['x'=4,'zh'=4,'zl'=4,'y'=4,'c'=2] {'zh'}, dimensions={0}, use_global_device_ids=true | all-gather | bytes 655360 | tf_op jit(solution)/shard_map/all_gather | solution.py:62
  81.9 1.2 fusion.4
  83.1 2.2 %fusion.5 = f32[512,128]{0,1:T(8,128)S(1)} fusion(f32[512,1024]{1,0:T(8,128)S(1)} %bitcast.62, f32[1024,128]{1,0:T(8,128)} %collective-permute-done.1), kind=kOutput, calls=%fused_computation.30 | convolution fusion | flops 402653184 | bytes 2883584 | tf_op jit(solution)/shard_map/dot_general | solution.py:33
  85.3 0.8 copy_bitcast_fusion
  86.1 6.0 %all-to-all-start.1 = ((f32[4,128,256]{1,2,0:T(8,128)}), f32[4,128,256]{1,2,0:T(8,128)S(1)}, u32[]{:S(2)}, u32[]{:S(2)}) async-start(f32[4,128,256]{1,2,0:T(8,128)} %copy_bitcast_fusion), calls=%async_computation.1 | async-start | bytes 1048576 | tf_op jit(solution)/shard_map/all_to_all | solution.py:68
  92.2 4.9 %collective-permute-start.4 = (f32[128,256]{1,0:T(8,128)S(1)}, f32[128,256]{1,0:T(8,128)S(1)}, u32[]{:S(2)}, u32[]{:S(2)}) collective-permute-start(f32[128,256]{1,0:T(8,128)S(1)} %get-tuple-element.31), channel_id=1, source_target_pairs={{0,6},{2,0},{4,2},{6,4},{1,7},{3,1},{5,3},{7,5},{8,14},{10,8},{12,... | collective-permute-start | bytes 393224 | tf_op jit(solution)/shard_map/ppermute | solution.py:73
  97.1 2.5 %collective-permute-start.3 = (f32[128,256]{1,0:T(8,128)S(1)}, f32[128,256]{1,0:T(8,128)S(1)}, u32[]{:S(2)}, u32[]{:S(2)}) collective-permute-start(f32[128,256]{1,0:T(8,128)S(1)} %get-tuple-element.32), channel_id=1, source_target_pairs={{0,4},{2,6},{4,0},{6,2},{1,5},{3,7},{5,1},{7,3},{8,12},{10,14},{12... | collective-permute-start | bytes 393224 | tf_op jit(solution)/shard_map/ppermute | solution.py:73
  99.5 2.5 %collective-permute-start.2 = (f32[128,256]{1,0:T(8,128)S(1)}, f32[128,256]{1,0:T(8,128)S(1)}, u32[]{:S(2)}, u32[]{:S(2)}) collective-permute-start(f32[128,256]{1,0:T(8,128)S(1)} %get-tuple-element.33), channel_id=1, source_target_pairs={{0,2},{2,4},{4,6},{6,0},{1,3},{3,5},{5,7},{7,1},{8,10},{10,12},{12... | collective-permute-start | bytes 393224 | tf_op jit(solution)/shard_map/ppermute | solution.py:73
  102.1 2.4 %collective-permute-done.3 = f32[128,256]{1,0:T(8,128)S(1)} collective-permute-done((f32[128,256]{1,0:T(8,128)S(1)}, f32[128,256]{1,0:T(8,128)S(1)}, u32[]{:S(2)}, u32[]{:S(2)}) %collective-permute-start.3) | collective-permute-done | bytes 131104 | tf_op jit(solution)/shard_map/ppermute | solution.py:73
  104.6 3.7 %collective-permute-done.2 = f32[128,256]{1,0:T(8,128)S(1)} collective-permute-done((f32[128,256]{1,0:T(8,128)S(1)}, f32[128,256]{1,0:T(8,128)S(1)}, u32[]{:S(2)}, u32[]{:S(2)}) %collective-permute-start.2) | collective-permute-done | bytes 131104 | tf_op jit(solution)/shard_map/ppermute | solution.py:73
  108.4 1.9 %collective-permute-start.5 = (f32[512,256]{1,0:T(8,128)S(1)}, f32[512,256]{1,0:T(8,128)S(1)}, u32[]{:S(2)}, u32[]{:S(2)}) collective-permute-start(f32[512,256]{1,0:T(8,128)S(1)} %pad_maximum_fusion.2), channel_id=1, source_target_pairs={{0,128},{128,0},{256,384},{384,256},{1,129},{129,1},{257,385},{385... | collective-permute-start | bytes 1572872 | tf_op jit(solution)/shard_map/ppermute | solution.py:78
  110.4 11.7 %collective-permute-done.5 = f32[512,256]{1,0:T(8,128)S(1)} collective-permute-done((f32[512,256]{1,0:T(8,128)S(1)}, f32[512,256]{1,0:T(8,128)S(1)}, u32[]{:S(2)}, u32[]{:S(2)}) %collective-permute-start.5) | collective-permute-done | bytes 524320 | tf_op jit(solution)/shard_map/ppermute | solution.py:78
  122.2 4.3 %all_gather.23 = f32[256,256]{0,1:T(8,128)S(1)} all-gather(f32[128,256]{0,1:T(8,128)S(1)} %maximum_select_fusion), channel_id=1, replica_groups=mesh['x'=4,'zh'=4,'zl'=4,'y'=4,'c'=2] {'c'}, dimensions={0}, use_global_device_ids=true | all-gather | bytes 393216 | tf_op jit(solution)/shard_map/all_gather | solution.py:83
  126.5 0.1 copy.37
  126.6 0.6 fusion
  127.3 16.8 %all_to_all.29 = f32[4,64,1024]{2,1,0:T(8,128)S(1)} all-to-all(f32[4,64,1024]{2,1,0:T(8,128)S(1)} %fusion), channel_id=1, replica_groups=mesh['x'=4,'zh'=4,'zl'=4,'y'=4,'c'=2] {'y'}, dimensions={0} | all-to-all | bytes 2097152 | tf_op jit(solution)/shard_map/all_to_all | solution.py:88
  144.1 0.8 reduce_sum.28
  144.9 6.1 %all-to-all-start.3 = ((f32[8,8,1024]{2,1,0:T(8,128)}), f32[8,8,1024]{2,1,0:T(8,128)S(1)}, u32[]{:S(2)}, u32[]{:S(2)}) async-start(f32[8,8,1024]{2,1,0:T(8,128)} %bitcast.21), calls=%async_computation.3 | async-start | bytes 524288 | tf_op jit(solution)/shard_map/all_to_all | solution.py:90
  151.0 0.8 copy.41
  151.8 7.9 %all-to-all-done.3 = f32[8,8,1024]{2,1,0:T(8,128)S(1)} async-done(((f32[8,8,1024]{2,1,0:T(8,128)}), f32[8,8,1024]{2,1,0:T(8,128)S(1)}, u32[]{:S(2)}, u32[]{:S(2)}) %all-to-all-start.3) | async-done | bytes 262176 | tf_op jit(solution)/shard_map/all_to_all | solution.py:90
  159.8 0.6 sub.15
  (25 shorter events, 0.4 us)
Async XLA Ops:
  0.6 19.9 %collective-permute-start = (f32[128,256]{1,0:T(8,128)}, f32[128,256]{1,0:T(8,128)S(1)}, u32[]{:S(2)}, u32[]{:S(2)}) collective-permute-start(f32[128,256]{1,0:T(8,128)} %param.4), channel_id=1, source_target_pairs={{0,0},{1,1},{2,2},{3,3},{4,4},{5,5},{6,6},{7,7},{8,128},{9,129},{1... | collective-permute-start | bytes 393224 | tf_op jit(solution)/shard_map/ppermute | solution.py:46
  35.1 46.8 %all-to-all-start = ((f32[4,128,1024]{2,1,0:T(8,128)}), f32[4,128,1024]{2,1,0:T(8,128)S(1)}, u32[]{:S(2)}, u32[]{:S(2)}) async-start(f32[4,128,1024]{2,1,0:T(8,128)} %stack.25), calls=%async_computation | async-start | bytes 4194304 | tf_op jit(solution)/shard_map/all_to_all | solution.py:59
  39.7 43.3 %collective-permute-start.1 = (f32[1024,128]{1,0:T(8,128)S(1)}, f32[1024,128]{1,0:T(8,128)}, u32[]{:S(2)}, u32[]{:S(2)}) collective-permute-start(f32[1024,128]{1,0:T(8,128)S(1)} %all_gather.18), channel_id=1, source_target_pairs={{0,1},{1,0},{2,3},{3,2},{4,5},{5,4},{6,7},{7,6},{8,9},{9,8},{10,11... | collective-permute-start | bytes 1572872 | tf_op jit(solution)/shard_map/ppermute | solution.py:53
  86.1 36.0 %all-to-all-start.1 = ((f32[4,128,256]{1,2,0:T(8,128)}), f32[4,128,256]{1,2,0:T(8,128)S(1)}, u32[]{:S(2)}, u32[]{:S(2)}) async-start(f32[4,128,256]{1,2,0:T(8,128)} %copy_bitcast_fusion), calls=%async_computation.1 | async-start | bytes 1048576 | tf_op jit(solution)/shard_map/all_to_all | solution.py:68
  92.2 9.9 %collective-permute-start.4 = (f32[128,256]{1,0:T(8,128)S(1)}, f32[128,256]{1,0:T(8,128)S(1)}, u32[]{:S(2)}, u32[]{:S(2)}) collective-permute-start(f32[128,256]{1,0:T(8,128)S(1)} %get-tuple-element.31), channel_id=1, source_target_pairs={{0,6},{2,0},{4,2},{6,4},{1,7},{3,1},{5,3},{7,5},{8,14},{10,8},{12,... | collective-permute-start | bytes 393224 | tf_op jit(solution)/shard_map/ppermute | solution.py:73
  97.1 7.5 %collective-permute-start.3 = (f32[128,256]{1,0:T(8,128)S(1)}, f32[128,256]{1,0:T(8,128)S(1)}, u32[]{:S(2)}, u32[]{:S(2)}) collective-permute-start(f32[128,256]{1,0:T(8,128)S(1)} %get-tuple-element.32), channel_id=1, source_target_pairs={{0,4},{2,6},{4,0},{6,2},{1,5},{3,7},{5,1},{7,3},{8,12},{10,14},{12... | collective-permute-start | bytes 393224 | tf_op jit(solution)/shard_map/ppermute | solution.py:73
  99.5 8.7 %collective-permute-start.2 = (f32[128,256]{1,0:T(8,128)S(1)}, f32[128,256]{1,0:T(8,128)S(1)}, u32[]{:S(2)}, u32[]{:S(2)}) collective-permute-start(f32[128,256]{1,0:T(8,128)S(1)} %get-tuple-element.33), channel_id=1, source_target_pairs={{0,2},{2,4},{4,6},{6,0},{1,3},{3,5},{5,7},{7,1},{8,10},{10,12},{12... | collective-permute-start | bytes 393224 | tf_op jit(solution)/shard_map/ppermute | solution.py:73
  108.4 13.6 %collective-permute-start.5 = (f32[512,256]{1,0:T(8,128)S(1)}, f32[512,256]{1,0:T(8,128)S(1)}, u32[]{:S(2)}, u32[]{:S(2)}) collective-permute-start(f32[512,256]{1,0:T(8,128)S(1)} %pad_maximum_fusion.2), channel_id=1, source_target_pairs={{0,128},{128,0},{256,384},{384,256},{1,129},{129,1},{257,385},{385... | collective-permute-start | bytes 1572872 | tf_op jit(solution)/shard_map/ppermute | solution.py:78
  144.1 15.7 %copy-start = (f32[8,2048]{1,0:T(8,128)S(1)}, f32[8,2048]{1,0:T(8,128)}, u32[]{:S(2)}) copy-start(f32[8,2048]{1,0:T(8,128)} %param.6) | copy-start | bytes 196612
  144.9 14.8 %all-to-all-start.3 = ((f32[8,8,1024]{2,1,0:T(8,128)}), f32[8,8,1024]{2,1,0:T(8,128)S(1)}, u32[]{:S(2)}, u32[]{:S(2)}) async-start(f32[8,8,1024]{2,1,0:T(8,128)} %bitcast.21), calls=%async_computation.3 | async-start | bytes 524288 | tf_op jit(solution)/shard_map/all_to_all | solution.py:90

commit v3 on v2

--- a/solution.py
+++ b/solution.py
@@ -49,11 +49,14 @@
     ).astype(jnp.float32)
     moved = moved * jnp.repeat(own, 128, axis=1)
 
-    a_own = lax.all_gather(ancestor_inverse, "x", axis=0, tiled=True)
-    a_other = lax.ppermute(a_own, "c", [(0, 1), (1, 0)])
+    a_cols = lax.all_gather(ancestor_inverse, "c", axis=0)
+    a_cols = jnp.concatenate([a_cols[0], a_cols[1]], axis=1)
+    a_copies = lax.optimization_barrier(jnp.stack([a_cols] * 4))
+    a_all = lax.all_to_all(a_copies, "x", 0, 0, tiled=True).reshape(1024, 256)
 
-    moved, a_own = lax.optimization_barrier((moved, a_own))
+    moved, _ = lax.optimization_barrier((moved, a_copies))
     over_zl = lax.all_gather(moved, "zl", axis=0)
+    over_zl, a_all = lax.optimization_barrier((over_zl, a_all))
     over_zl = over_zl.transpose(1, 0, 2).reshape(128, 1024)
     copies = lax.optimization_barrier(jnp.stack([over_zl] * 4))
     by_y = lax.all_to_all(copies, "y", 0, 0, tiled=True).reshape(512, 1024)
@@ -61,26 +64,24 @@
     moved, _ = lax.optimization_barrier((moved, copies))
     over_zh = lax.all_gather(moved, "zh", axis=0)
     by_y, over_zh = lax.optimization_barrier((by_y, over_zh))
+    pair_zh = lax.ppermute(over_zh, "x", [(i, i ^ 1) for i in range(4)])
 
-    partial = jnp.concatenate(
-        [dot(by_y, a, ((1,), (0,))) for a in (a_own, a_other)], axis=1
-    )
+    partial = dot(by_y, a_all, ((1,), (0,)))
     summed = lax.all_to_all(partial, "zh", 0, 0, tiled=True)
     summed = -jnp.sum(summed.reshape(4, 128, 256), axis=0)
 
-    over_zh, _ = lax.optimization_barrier((over_zh, partial))
-    pieces = [pick(over_zh, y)] + [
-        lax.ppermute(pick(over_zh, (y + s) % 4), "y", shift_pairs(s))
-        for s in (1, 2, 3)
+    def column(index):
+        return jnp.concatenate([pick(over_zh, index), pick(pair_zh, index)])
+
+    over_zh, pair_zh, _ = lax.optimization_barrier((over_zh, pair_zh, partial))
+    pieces = [column(y)] + [
+        lax.ppermute(column((y + s) % 4), "y", shift_pairs(s)) for s in (1, 2, 3)
     ]
-    pieces = jnp.stack(pieces)
-    col_half = jnp.concatenate([pick(pieces, (y - b) % 4) for b in range(4)])
-    col_other = lax.ppermute(col_half, "x", [(i, i ^ 1) for i in range(4)])
-    col_form = jnp.concatenate([col_half, col_other], axis=0)
+    pieces = jnp.stack(pieces).reshape(4, 2, 128, 256)
+    col_form = jnp.stack([pick(pieces, (y - b) % 4) for b in range(4)], axis=1)
+    col_form = col_form.reshape(1024, 256)
 
-    crossed = jnp.concatenate([summed[:, 128:], summed[:, :128]], axis=1)
-    half_rows = jnp.where(c == 0, summed, crossed)
-    rows = lax.all_gather(half_rows, "c", axis=0, tiled=True)
+    rows = lax.all_gather(summed, "c", axis=0, tiled=True)
     inverse_rows = lax.dynamic_slice_in_dim(rows, c * 128, 128, 1)
 
     lhs = rows.reshape(4, 4, 16, 256).transpose(1, 0, 2, 3).reshape(256, 256)

time: 161 us -> 153 us (0.950)
  waiting for transfers between devices: 25.7 us -> 16.1 us
  blocking collectives: 86.3 us -> 89 us
  local copies, waits for them, and re-layouts: 3.19 us -> 5.34 us
    ppermute x5 -> x4, waiting for transfers between devices: 17.8 us -> 6.58 us  [the longest x3 6.58 us: on_device(): lax.ppermute(column((y + s) % 4), 'y', shift_pairs(s))]
    all_gather x1, blocking collectives: 12.5 us -> 22.8 us  [on_device(): over_zl = lax.all_gather(moved, 'zl', axis=0)]
    ppermute x5 -> x4, starting transfers between devices: 18.7 us -> 9.7 us  [the longest x3 7.7 us: on_device(): lax.ppermute(column((y + s) % 4), 'y', shift_pairs(s))]
    all_gather x1, blocking collectives: 35.2 us -> 27.3 us  [on_device(): over_zh = lax.all_gather(moved, 'zh', axis=0)]
    all_to_all x1, starting transfers between devices: 6.02 us -> 10.9 us  [on_device(): summed = lax.all_to_all(partial, 'zh', 0, 0, tiled=True)]
    all_to_all x0 -> x1, starting transfers between devices: none -> 3.51 us  [on_device(): a_all = lax.all_to_all(a_copies, 'x', 0, 0, tiled=True).reshape(1024, 256)]
    dot_general x3 -> x2, matrix products: 4 us -> 2.42 us  [dot(): lax.dot_general(lhs, rhs, (dims, ((), ())), precision=high, preferred_ele...]
  transfers between devices with their start and end apart: 9 -> 9, of which waited for: 4 -> 4; matrix products, arithmetic and copies ran while one was open for 2% -> 3% of each run, Pallas kernels for 0% -> 0%
where the time goes in v3:
time: 153 us; the launch traced here: 152 us
  blocking collectives  89 us (58%)
  starting transfers between devices  35.9 us (23%)
  waiting for transfers between devices  16.1 us (11%)
  local copies, waits for them, and re-layouts  5.34 us (3%)
  other arithmetic  2.57 us (2%)
  matrix products  2.42 us (2%)
    all_gather x1, blocking collectives, on_device(): over_zh = lax.all_gather(moved, 'zh', axis=0)  27.3 us
    all_gather x1, blocking collectives, on_device(): over_zl = lax.all_gather(moved, 'zl', axis=0)  22.8 us
    all_to_all x1, blocking collectives, on_device(): over_y = lax.all_to_all(coupling, 'y', 0, 0, tiled=True)  18.1 us
    all_gather x1, blocking collectives, on_device(): rows = lax.all_gather(summed, 'c', axis=0, tiled=True)  12.1 us
    all_to_all x1, starting transfers between devices, on_device(): summed = lax.all_to_all(partial, 'zh', 0, 0, tiled=True)  10.9 us
    all_gather x1, blocking collectives, on_device(): a_cols = lax.all_gather(ancestor_inverse, 'c', axis=0)  8.72 us
    all_to_all x1, waiting for transfers between devices, on_device(): over_l = lax.all_to_all(sum_y, ('zl', 'c'), 0, 0, tiled=True)  8.04 us
    ppermute x3, starting transfers between devices, on_device(): lax.ppermute(column((y + s) % 4), 'y', shift_pairs(s))  7.7 us
  transfers between devices with their start and end apart: 9, of which 4 were waited for; matrix products, arithmetic and copies ran while one was open for 3% of the time, Pallas kernels for 0%

profile of v3, /device:TPU:1, one launch (start us, length us, event | category | flops | bytes accessed | tf_op | source)
XLA Modules:
  0.0 152.3 jit_solution(15393305861449353637)
XLA Ops:
  0.6 8.7 %all-gather = f32[512,128]{1,0:T(8,128)S(1)} all-gather(f32[256,128]{1,0:T(8,128)} %param.5), channel_id=2, replica_groups=mesh['x'=4,'zh'=4,'zl'=4,'y'=4,'c'=2] {'c'}, dimensions={0}, use_global_device_ids=true | all-gather | bytes 393216 | tf_op jit(solution)/shard_map/all_gather | solution.py:52
  9.4 1.1 stack.49
  10.5 3.5 %all-to-all-start = ((f32[4,256,256]{2,1,0:T(8,128)}), f32[4,256,256]{2,1,0:T(8,128)S(1)}, u32[]{:S(2)}, u32[]{:S(2)}) async-start(f32[4,256,256]{2,1,0:T(8,128)} %stack.49), calls=%async_computation | async-start | bytes 2097152 | tf_op jit(solution)/shard_map/all_to_all | solution.py:55
  14.0 0.7 collective-permute-start
  14.7 0.8 convert_bitcast_fusion
  15.6 22.8 %all-gather.1 = f32[512,256]{1,0:T(8,128)S(1)} all-gather(f32[128,256]{1,0:T(8,128)S(1)} %broadcast_multiply_fusion), channel_id=3, replica_groups=mesh['x'=4,'zh'=4,'zl'=4,'y'=4,'c'=2] {'zl'}, dimensions={0}, use_global_device_ids=true | all-gather | bytes 655360 | tf_op jit(solution)/shard_map/all_gather | solution.py:58
  38.4 0.2 copy.16
  38.5 0.2 copy.17
  38.8 1.6 %stack.50 = f32[4,128,1024]{2,1,0:T(8,128)} broadcast(f32[128,1024]{1,0:T(8,128)S(1)} %copy.17), dimensions={1,2} | broadcast | bytes 2621440 | tf_op jit(solution)/shard_map/stack | solution.py:61
  40.4 3.6 %all-to-all-start.1 = ((f32[4,128,1024]{2,1,0:T(8,128)}), f32[4,128,1024]{2,1,0:T(8,128)S(1)}, u32[]{:S(2)}, u32[]{:S(2)}) async-start(f32[4,128,1024]{2,1,0:T(8,128)} %stack.50), calls=%async_computation.1 | async-start | bytes 4194304 | tf_op jit(solution)/shard_map/all_to_all | solution.py:62
  44.0 27.3 %all-gather.2 = f32[512,256]{1,0:T(8,128)} all-gather(f32[128,256]{1,0:T(8,128)S(1)} %broadcast_multiply_fusion), channel_id=4, replica_groups=mesh['x'=4,'zh'=4,'zl'=4,'y'=4,'c'=2] {'zh'}, dimensions={0}, use_global_device_ids=true | all-gather | bytes 655360 | tf_op jit(solution)/shard_map/all_gather | solution.py:65
  71.2 2.0 %collective-permute-start.1 = (f32[4,128,256]{2,1,0:T(8,128)}, f32[4,128,256]{2,1,0:T(8,128)}, u32[]{:S(2)}, u32[]{:S(2)}) collective-permute-start(f32[4,128,256]{2,1,0:T(8,128)} %bitcast.66), channel_id=1, source_target_pairs={{0,128},{128,0},{256,384},{384,256},{1,129},{129,1},{257,385},{385... | collective-permute-start | bytes 1572872 | tf_op jit(solution)/shard_map/ppermute | solution.py:67
  73.3 1.8 %fusion.1 = f32[512,256]{1,0:T(8,128)} fusion(f32[512,1024]{1,0:T(8,128)S(1)} %bitcast.63, f32[1024,256]{1,0:T(8,128)S(1)} %bitcast.64), kind=kOutput, calls=%fused_computation.27 | convolution fusion | flops 805306368 | bytes 3670016 | tf_op jit(solution)/shard_map/dot_general | solution.py:33
  75.0 10.9 %all-to-all-start.2 = ((f32[4,128,256]{2,1,0:T(8,128)}), f32[4,128,256]{2,1,0:T(8,128)S(1)}, u32[]{:S(2)}, u32[]{:S(2)}) async-start(f32[4,128,256]{2,1,0:T(8,128)} %bitcast.68), calls=%async_computation.2 | async-start | bytes 1048576 | tf_op jit(solution)/shard_map/all_to_all | solution.py:70
  86.0 1.4 dynamic-slice_bitcast_fusion.10
  87.4 2.7 %collective-permute-start.4 = (f32[256,256]{1,0:T(8,128)S(1)}, f32[256,256]{1,0:T(8,128)S(1)}, u32[]{:S(2)}, u32[]{:S(2)}) collective-permute-start(f32[256,256]{1,0:T(8,128)S(1)} %pad_maximum_fusion.6), channel_id=1, source_target_pairs={{0,6},{2,0},{4,2},{6,4},{1,7},{3,1},{5,3},{7,5},{8,14},{10,8},{12,... | collective-permute-start | bytes 786440 | tf_op jit(solution)/shard_map/ppermute | solution.py:78
  90.1 3.1 %collective-permute-start.3 = (f32[256,256]{1,0:T(8,128)S(1)}, f32[256,256]{1,0:T(8,128)S(1)}, u32[]{:S(2)}, u32[]{:S(2)}) collective-permute-start(f32[256,256]{1,0:T(8,128)S(1)} %pad_maximum_fusion.5), channel_id=1, source_target_pairs={{0,4},{2,6},{4,0},{6,2},{1,5},{3,7},{5,1},{7,3},{8,12},{10,14},{12... | collective-permute-start | bytes 786440 | tf_op jit(solution)/shard_map/ppermute | solution.py:78
  93.2 1.9 %collective-permute-start.2 = (f32[256,256]{1,0:T(8,128)S(1)}, f32[256,256]{1,0:T(8,128)S(1)}, u32[]{:S(2)}, u32[]{:S(2)}) collective-permute-start(f32[256,256]{1,0:T(8,128)S(1)} %pad_maximum_fusion.4), channel_id=1, source_target_pairs={{0,2},{2,4},{4,6},{6,0},{1,3},{3,5},{5,7},{7,1},{8,10},{10,12},{12... | collective-permute-start | bytes 786440 | tf_op jit(solution)/shard_map/ppermute | solution.py:78
  95.3 3.7 %collective-permute-done.3 = f32[256,256]{1,0:T(8,128)S(1)} collective-permute-done((f32[256,256]{1,0:T(8,128)S(1)}, f32[256,256]{1,0:T(8,128)S(1)}, u32[]{:S(2)}, u32[]{:S(2)}) %collective-permute-start.3) | collective-permute-done | bytes 262176 | tf_op jit(solution)/shard_map/ppermute | solution.py:78
  99.0 2.8 %collective-permute-done.2 = f32[256,256]{1,0:T(8,128)S(1)} collective-permute-done((f32[256,256]{1,0:T(8,128)S(1)}, f32[256,256]{1,0:T(8,128)S(1)}, u32[]{:S(2)}, u32[]{:S(2)}) %collective-permute-start.2) | collective-permute-done | bytes 262176 | tf_op jit(solution)/shard_map/ppermute | solution.py:78
  101.9 0.1 pad_maximum_fusion
  102.0 0.1 dynamic-slice_bitcast_fusion.3
  102.1 0.1 pad_maximum_fusion.1
  102.2 1.5 all-to-all-done.2
  103.7 12.1 %all_gather.27 = f32[256,256]{1,0:T(8,128)S(1)} all-gather(f32[128,256]{1,0:T(8,128)S(1)} %neg.3), channel_id=1, replica_groups=mesh['x'=4,'zh'=4,'zl'=4,'y'=4,'c'=2] {'c'}, dimensions={0}, use_global_device_ids=true | all-gather | bytes 393216 | tf_op jit(solution)/shard_map/all_gather | solution.py:84
  115.9 0.6 fusion.2
  116.5 18.1 %all_to_all.34 = f32[4,64,1024]{2,1,0:T(8,128)S(1)} all-to-all(f32[4,64,1024]{2,1,0:T(8,128)S(1)} %fusion.2), channel_id=1, replica_groups=mesh['x'=4,'zh'=4,'zl'=4,'y'=4,'c'=2] {'y'}, dimensions={0} | all-to-all | bytes 2097152 | tf_op jit(solution)/shard_map/all_to_all | solution.py:89
  134.6 0.8 reduce_sum.28
  135.4 7.5 %all-to-all-start.4 = ((f32[8,8,1024]{2,1,0:T(8,128)}), f32[8,8,1024]{2,1,0:T(8,128)S(1)}, u32[]{:S(2)}, u32[]{:S(2)}) async-start(f32[8,8,1024]{2,1,0:T(8,128)} %bitcast.30), calls=%async_computation.4 | async-start | bytes 524288 | tf_op jit(solution)/shard_map/all_to_all | solution.py:91
  142.9 0.7 constant_dynamic-slice_fusion
  143.6 8.0 %all-to-all-done.4 = f32[8,8,1024]{2,1,0:T(8,128)S(1)} async-done(((f32[8,8,1024]{2,1,0:T(8,128)}), f32[8,8,1024]{2,1,0:T(8,128)S(1)}, u32[]{:S(2)}, u32[]{:S(2)}) %all-to-all-start.4) | async-done | bytes 262176 | tf_op jit(solution)/shard_map/all_to_all | solution.py:91
  151.7 0.6 sub.15
  (24 shorter events, 0.3 us)
Async XLA Ops:
  9.4 4.6 %copy-start.1 = (f32[128,256]{1,0:T(8,128)S(1)}, f32[128,256]{1,0:T(8,128)}, u32[]{:S(2)}) copy-start(f32[128,256]{1,0:T(8,128)} %param.4) | copy-start | bytes 393220
  10.5 27.9 %all-to-all-start = ((f32[4,256,256]{2,1,0:T(8,128)}), f32[4,256,256]{2,1,0:T(8,128)S(1)}, u32[]{:S(2)}, u32[]{:S(2)}) async-start(f32[4,256,256]{2,1,0:T(8,128)} %stack.49), calls=%async_computation | async-start | bytes 2097152 | tf_op jit(solution)/shard_map/all_to_all | solution.py:55
  14.0 1.5 %collective-permute-start = (f32[128,256]{1,0:T(8,128)S(1)}, f32[128,256]{1,0:T(8,128)S(1)}, u32[]{:S(2)}, u32[]{:S(2)}) collective-permute-start(f32[128,256]{1,0:T(8,128)S(1)} %copy-done.1), channel_id=1, source_target_pairs={{0,0},{1,1},{2,2},{3,3},{4,4},{5,5},{6,6},{7,7},{8,128},{9,129},{1... | collective-permute-start | bytes 393224 | tf_op jit(solution)/shard_map/ppermute | solution.py:46
  40.4 30.9 %all-to-all-start.1 = ((f32[4,128,1024]{2,1,0:T(8,128)}), f32[4,128,1024]{2,1,0:T(8,128)S(1)}, u32[]{:S(2)}, u32[]{:S(2)}) async-start(f32[4,128,1024]{2,1,0:T(8,128)} %stack.50), calls=%async_computation.1 | async-start | bytes 4194304 | tf_op jit(solution)/shard_map/all_to_all | solution.py:62
  71.2 14.7 %collective-permute-start.1 = (f32[4,128,256]{2,1,0:T(8,128)}, f32[4,128,256]{2,1,0:T(8,128)}, u32[]{:S(2)}, u32[]{:S(2)}) collective-permute-start(f32[4,128,256]{2,1,0:T(8,128)} %bitcast.66), channel_id=1, source_target_pairs={{0,128},{128,0},{256,384},{384,256},{1,129},{129,1},{257,385},{385... | collective-permute-start | bytes 1572872 | tf_op jit(solution)/shard_map/ppermute | solution.py:67
  75.0 28.6 %all-to-all-start.2 = ((f32[4,128,256]{2,1,0:T(8,128)}), f32[4,128,256]{2,1,0:T(8,128)S(1)}, u32[]{:S(2)}, u32[]{:S(2)}) async-start(f32[4,128,256]{2,1,0:T(8,128)} %bitcast.68), calls=%async_computation.2 | async-start | bytes 1048576 | tf_op jit(solution)/shard_map/all_to_all | solution.py:70
  87.4 7.9 %collective-permute-start.4 = (f32[256,256]{1,0:T(8,128)S(1)}, f32[256,256]{1,0:T(8,128)S(1)}, u32[]{:S(2)}, u32[]{:S(2)}) collective-permute-start(f32[256,256]{1,0:T(8,128)S(1)} %pad_maximum_fusion.6), channel_id=1, source_target_pairs={{0,6},{2,0},{4,2},{6,4},{1,7},{3,1},{5,3},{7,5},{8,14},{10,8},{12,... | collective-permute-start | bytes 786440 | tf_op jit(solution)/shard_map/ppermute | solution.py:78
  90.1 8.9 %collective-permute-start.3 = (f32[256,256]{1,0:T(8,128)S(1)}, f32[256,256]{1,0:T(8,128)S(1)}, u32[]{:S(2)}, u32[]{:S(2)}) collective-permute-start(f32[256,256]{1,0:T(8,128)S(1)} %pad_maximum_fusion.5), channel_id=1, source_target_pairs={{0,4},{2,6},{4,0},{6,2},{1,5},{3,7},{5,1},{7,3},{8,12},{10,14},{12... | collective-permute-start | bytes 786440 | tf_op jit(solution)/shard_map/ppermute | solution.py:78
  93.2 8.6 %collective-permute-start.2 = (f32[256,256]{1,0:T(8,128)S(1)}, f32[256,256]{1,0:T(8,128)S(1)}, u32[]{:S(2)}, u32[]{:S(2)}) collective-permute-start(f32[256,256]{1,0:T(8,128)S(1)} %pad_maximum_fusion.4), channel_id=1, source_target_pairs={{0,2},{2,4},{4,6},{6,0},{1,3},{3,5},{5,7},{7,1},{8,10},{10,12},{12... | collective-permute-start | bytes 786440 | tf_op jit(solution)/shard_map/ppermute | solution.py:78
  116.5 35.2 %copy-start = (f32[8,2048]{1,0:T(8,128)S(1)}, f32[8,2048]{1,0:T(8,128)}, u32[]{:S(2)}) copy-start(f32[8,2048]{1,0:T(8,128)} %param.6) | copy-start | bytes 196612
  135.4 16.2 %all-to-all-start.4 = ((f32[8,8,1024]{2,1,0:T(8,128)}), f32[8,8,1024]{2,1,0:T(8,128)S(1)}, u32[]{:S(2)}, u32[]{:S(2)}) async-start(f32[8,8,1024]{2,1,0:T(8,128)} %bitcast.30), calls=%async_computation.4 | async-start | bytes 524288 | tf_op jit(solution)/shard_map/all_to_all | solution.py:91

commit v4 on v3

--- a/solution.py
+++ b/solution.py
@@ -51,10 +51,9 @@
 
     a_cols = lax.all_gather(ancestor_inverse, "c", axis=0)
     a_cols = jnp.concatenate([a_cols[0], a_cols[1]], axis=1)
-    a_copies = lax.optimization_barrier(jnp.stack([a_cols] * 4))
+    a_copies, moved = lax.optimization_barrier((jnp.stack([a_cols] * 4), moved))
     a_all = lax.all_to_all(a_copies, "x", 0, 0, tiled=True).reshape(1024, 256)
 
-    moved, _ = lax.optimization_barrier((moved, a_copies))
     over_zl = lax.all_gather(moved, "zl", axis=0)
     over_zl, a_all = lax.optimization_barrier((over_zl, a_all))
     over_zl = over_zl.transpose(1, 0, 2).reshape(128, 1024)

time: 153 us -> 150 us (0.980)
  blocking collectives: 89 us -> 87 us
    all_gather x1, blocking collectives: 22.8 us -> 13.9 us  [on_device(): over_zl = lax.all_gather(moved, 'zl', axis=0)]
    all_to_all x1, starting transfers between devices: 10.9 us -> 6.37 us  [on_device(): summed = lax.all_to_all(partial, 'zh', 0, 0, tiled=True)]
    all_gather x1, blocking collectives: 27.3 us -> 31 us  [on_device(): over_zh = lax.all_gather(moved, 'zh', axis=0)]
    all_to_all x1, starting transfers between devices: 3.51 us -> 6.7 us  [on_device(): a_all = lax.all_to_all(a_copies, 'x', 0, 0, tiled=True).reshape(1024, 256)]
    all_to_all x1, starting transfers between devices: 7.51 us -> 5.11 us  [on_device(): over_l = lax.all_to_all(sum_y, ('zl', 'c'), 0, 0, tiled=True)]
    all_to_all x1, blocking collectives: 18.1 us -> 20.2 us  [on_device(): over_y = lax.all_to_all(coupling, 'y', 0, 0, tiled=True)]
  transfers between devices with their start and end apart: 9 -> 9, of which waited for: 4 -> 3; matrix products, arithmetic and copies ran while one was open for 3% -> 3% of each run, Pallas kernels for 0% -> 0%
where the time goes in v4:
time: 150 us
  blocking collectives  87 us (58%)
  starting transfers between devices  36.6 us (24%)
  waiting for transfers between devices  14.7 us (10%)
  local copies, waits for them, and re-layouts  5.33 us (4%)
  other arithmetic  2.56 us (2%)
  matrix products  2.42 us (2%)
    all_gather x1, blocking collectives, on_device(): over_zh = lax.all_gather(moved, 'zh', axis=0)  31 us
    all_to_all x1, blocking collectives, on_device(): over_y = lax.all_to_all(coupling, 'y', 0, 0, tiled=True)  20.2 us
    all_gather x1, blocking collectives, on_device(): over_zl = lax.all_gather(moved, 'zl', axis=0)  13.9 us
    all_gather x1, blocking collectives, on_device(): rows = lax.all_gather(summed, 'c', axis=0, tiled=True)  13.2 us
    ppermute x3, starting transfers between devices, on_device(): lax.ppermute(column((y + s) % 4), 'y', shift_pairs(s))  9.19 us
    all_gather x1, blocking collectives, on_device(): a_cols = lax.all_gather(ancestor_inverse, 'c', axis=0)  8.71 us
    all_to_all x1, waiting for transfers between devices, on_device(): over_l = lax.all_to_all(sum_y, ('zl', 'c'), 0, 0, tiled=True)  8.06 us
    all_to_all x1, starting transfers between devices, on_device(): a_all = lax.all_to_all(a_copies, 'x', 0, 0, tiled=True).reshape(1024, 256)  6.7 us
  transfers between devices with their start and end apart: 9, of which 3 were waited for; matrix products, arithmetic and copies ran while one was open for 3% of the time, Pallas kernels for 0%

profile of v4, /device:TPU:1, one launch (start us, length us, event | category | flops | bytes accessed | tf_op | source)
XLA Modules:
  0.0 149.5 jit_solution(15535547350767895716)
XLA Ops:
  0.6 1.6 %collective-permute-start = (f32[128,256]{1,0:T(8,128)}, f32[128,256]{1,0:T(8,128)S(1)}, u32[]{:S(2)}, u32[]{:S(2)}) collective-permute-start(f32[128,256]{1,0:T(8,128)} %param.4), channel_id=1, source_target_pairs={{0,0},{1,1},{2,2},{3,3},{4,4},{5,5},{6,6},{7,7},{8,128},{9,129},{1... | collective-permute-start | bytes 393224 | tf_op jit(solution)/shard_map/ppermute | solution.py:46
  2.2 8.7 %all-gather = f32[512,128]{1,0:T(8,128)S(1)} all-gather(f32[256,128]{1,0:T(8,128)} %param.5), channel_id=2, replica_groups=mesh['x'=4,'zh'=4,'zl'=4,'y'=4,'c'=2] {'c'}, dimensions={0}, use_global_device_ids=true | all-gather | bytes 393216 | tf_op jit(solution)/shard_map/all_gather | solution.py:52
  10.9 0.8 convert_bitcast_fusion
  11.7 0.1 broadcast_bitcast_fusion
  11.8 1.0 stack.49
  12.9 6.7 %all-to-all-start = ((f32[4,256,256]{2,1,0:T(8,128)}), f32[4,256,256]{2,1,0:T(8,128)S(1)}, u32[]{:S(2)}, u32[]{:S(2)}) async-start(f32[4,256,256]{2,1,0:T(8,128)} %stack.49), calls=%async_computation | async-start | bytes 2097152 | tf_op jit(solution)/shard_map/all_to_all | solution.py:55
  19.6 13.9 %all-gather.1 = f32[512,256]{1,0:T(8,128)S(1)} all-gather(f32[128,256]{1,0:T(8,128)S(1)} %broadcast_multiply_fusion), channel_id=3, replica_groups=mesh['x'=4,'zh'=4,'zl'=4,'y'=4,'c'=2] {'zl'}, dimensions={0}, use_global_device_ids=true | all-gather | bytes 655360 | tf_op jit(solution)/shard_map/all_gather | solution.py:57
  33.5 0.2 copy.16
  33.7 0.2 copy.17
  33.9 1.6 %stack.50 = f32[4,128,1024]{2,1,0:T(8,128)} broadcast(f32[128,1024]{1,0:T(8,128)S(1)} %copy.17), dimensions={1,2} | broadcast | bytes 2621440 | tf_op jit(solution)/shard_map/stack | solution.py:60
  35.5 4.2 %all-to-all-start.1 = ((f32[4,128,1024]{2,1,0:T(8,128)}), f32[4,128,1024]{2,1,0:T(8,128)S(1)}, u32[]{:S(2)}, u32[]{:S(2)}) async-start(f32[4,128,1024]{2,1,0:T(8,128)} %stack.50), calls=%async_computation.1 | async-start | bytes 4194304 | tf_op jit(solution)/shard_map/all_to_all | solution.py:61
  39.7 31.0 %all-gather.2 = f32[512,256]{1,0:T(8,128)} all-gather(f32[128,256]{1,0:T(8,128)S(1)} %broadcast_multiply_fusion), channel_id=4, replica_groups=mesh['x'=4,'zh'=4,'zl'=4,'y'=4,'c'=2] {'zh'}, dimensions={0}, use_global_device_ids=true | all-gather | bytes 655360 | tf_op jit(solution)/shard_map/all_gather | solution.py:64
  70.7 3.5 %collective-permute-start.1 = (f32[4,128,256]{2,1,0:T(8,128)}, f32[4,128,256]{2,1,0:T(8,128)}, u32[]{:S(2)}, u32[]{:S(2)}) collective-permute-start(f32[4,128,256]{2,1,0:T(8,128)} %bitcast.66), channel_id=1, source_target_pairs={{0,128},{128,0},{256,384},{384,256},{1,129},{129,1},{257,385},{385... | collective-permute-start | bytes 1572872 | tf_op jit(solution)/shard_map/ppermute | solution.py:66
  74.2 1.8 %fusion.1 = f32[512,256]{1,0:T(8,128)} fusion(f32[512,1024]{1,0:T(8,128)S(1)} %bitcast.63, f32[1024,256]{1,0:T(8,128)S(1)} %bitcast.64), kind=kOutput, calls=%fused_computation.27 | convolution fusion | flops 805306368 | bytes 3670016 | tf_op jit(solution)/shard_map/dot_general | solution.py:33
  76.0 6.4 %all-to-all-start.2 = ((f32[4,128,256]{2,1,0:T(8,128)}), f32[4,128,256]{2,1,0:T(8,128)S(1)}, u32[]{:S(2)}, u32[]{:S(2)}) async-start(f32[4,128,256]{2,1,0:T(8,128)} %bitcast.68), calls=%async_computation.2 | async-start | bytes 1048576 | tf_op jit(solution)/shard_map/all_to_all | solution.py:69
  82.3 1.4 dynamic-slice_bitcast_fusion.10
  83.8 4.2 %collective-permute-start.4 = (f32[256,256]{1,0:T(8,128)S(1)}, f32[256,256]{1,0:T(8,128)S(1)}, u32[]{:S(2)}, u32[]{:S(2)}) collective-permute-start(f32[256,256]{1,0:T(8,128)S(1)} %pad_maximum_fusion.6), channel_id=1, source_target_pairs={{0,6},{2,0},{4,2},{6,4},{1,7},{3,1},{5,3},{7,5},{8,14},{10,8},{12,... | collective-permute-start | bytes 786440 | tf_op jit(solution)/shard_map/ppermute | solution.py:77
  88.0 2.5 %collective-permute-start.3 = (f32[256,256]{1,0:T(8,128)S(1)}, f32[256,256]{1,0:T(8,128)S(1)}, u32[]{:S(2)}, u32[]{:S(2)}) collective-permute-start(f32[256,256]{1,0:T(8,128)S(1)} %pad_maximum_fusion.5), channel_id=1, source_target_pairs={{0,4},{2,6},{4,0},{6,2},{1,5},{3,7},{5,1},{7,3},{8,12},{10,14},{12... | collective-permute-start | bytes 786440 | tf_op jit(solution)/shard_map/ppermute | solution.py:77
  90.5 2.5 %collective-permute-start.2 = (f32[256,256]{1,0:T(8,128)S(1)}, f32[256,256]{1,0:T(8,128)S(1)}, u32[]{:S(2)}, u32[]{:S(2)}) collective-permute-start(f32[256,256]{1,0:T(8,128)S(1)} %pad_maximum_fusion.4), channel_id=1, source_target_pairs={{0,2},{2,4},{4,6},{6,0},{1,3},{3,5},{5,7},{7,1},{8,10},{10,12},{12... | collective-permute-start | bytes 786440 | tf_op jit(solution)/shard_map/ppermute | solution.py:77
  93.1 3.8 %collective-permute-done.3 = f32[256,256]{1,0:T(8,128)S(1)} collective-permute-done((f32[256,256]{1,0:T(8,128)S(1)}, f32[256,256]{1,0:T(8,128)S(1)}, u32[]{:S(2)}, u32[]{:S(2)}) %collective-permute-start.3) | collective-permute-done | bytes 262176 | tf_op jit(solution)/shard_map/ppermute | solution.py:77
  96.9 2.8 %collective-permute-done.2 = f32[256,256]{1,0:T(8,128)S(1)} collective-permute-done((f32[256,256]{1,0:T(8,128)S(1)}, f32[256,256]{1,0:T(8,128)S(1)}, u32[]{:S(2)}, u32[]{:S(2)}) %collective-permute-start.2) | collective-permute-done | bytes 262176 | tf_op jit(solution)/shard_map/ppermute | solution.py:77
  99.7 0.1 pad_maximum_fusion
  99.9 0.1 dynamic-slice_bitcast_fusion.3
  100.0 0.1 pad_maximum_fusion.1
  100.1 13.2 %all_gather.27 = f32[256,256]{1,0:T(8,128)S(1)} all-gather(f32[128,256]{1,0:T(8,128)S(1)} %neg.3), channel_id=1, replica_groups=mesh['x'=4,'zh'=4,'zl'=4,'y'=4,'c'=2] {'c'}, dimensions={0}, use_global_device_ids=true | all-gather | bytes 393216 | tf_op jit(solution)/shard_map/all_gather | solution.py:83
  113.3 0.6 fusion.2
  114.0 20.2 %all_to_all.34 = f32[4,64,1024]{2,1,0:T(8,128)S(1)} all-to-all(f32[4,64,1024]{2,1,0:T(8,128)S(1)} %fusion.2), channel_id=1, replica_groups=mesh['x'=4,'zh'=4,'zl'=4,'y'=4,'c'=2] {'y'}, dimensions={0} | all-to-all | bytes 2097152 | tf_op jit(solution)/shard_map/all_to_all | solution.py:88
  134.2 0.8 reduce_sum.28
  135.0 5.1 %all-to-all-start.4 = ((f32[8,8,1024]{2,1,0:T(8,128)}), f32[8,8,1024]{2,1,0:T(8,128)S(1)}, u32[]{:S(2)}, u32[]{:S(2)}) async-start(f32[8,8,1024]{2,1,0:T(8,128)} %bitcast.30), calls=%async_computation.4 | async-start | bytes 524288 | tf_op jit(solution)/shard_map/all_to_all | solution.py:90
  140.1 0.7 constant_dynamic-slice_fusion
  140.7 8.1 %all-to-all-done.4 = f32[8,8,1024]{2,1,0:T(8,128)S(1)} async-done(((f32[8,8,1024]{2,1,0:T(8,128)}), f32[8,8,1024]{2,1,0:T(8,128)S(1)}, u32[]{:S(2)}, u32[]{:S(2)}) %all-to-all-start.4) | async-done | bytes 262176 | tf_op jit(solution)/shard_map/all_to_all | solution.py:90
  148.9 0.6 sub.15
  (22 shorter events, 0.3 us)
Async XLA Ops:
  0.6 11.2 %collective-permute-start = (f32[128,256]{1,0:T(8,128)}, f32[128,256]{1,0:T(8,128)S(1)}, u32[]{:S(2)}, u32[]{:S(2)}) collective-permute-start(f32[128,256]{1,0:T(8,128)} %param.4), channel_id=1, source_target_pairs={{0,0},{1,1},{2,2},{3,3},{4,4},{5,5},{6,6},{7,7},{8,128},{9,129},{1... | collective-permute-start | bytes 393224 | tf_op jit(solution)/shard_map/ppermute | solution.py:46
  12.9 20.6 %all-to-all-start = ((f32[4,256,256]{2,1,0:T(8,128)}), f32[4,256,256]{2,1,0:T(8,128)S(1)}, u32[]{:S(2)}, u32[]{:S(2)}) async-start(f32[4,256,256]{2,1,0:T(8,128)} %stack.49), calls=%async_computation | async-start | bytes 2097152 | tf_op jit(solution)/shard_map/all_to_all | solution.py:55
  35.5 35.2 %all-to-all-start.1 = ((f32[4,128,1024]{2,1,0:T(8,128)}), f32[4,128,1024]{2,1,0:T(8,128)S(1)}, u32[]{:S(2)}, u32[]{:S(2)}) async-start(f32[4,128,1024]{2,1,0:T(8,128)} %stack.50), calls=%async_computation.1 | async-start | bytes 4194304 | tf_op jit(solution)/shard_map/all_to_all | solution.py:61
  70.7 11.7 %collective-permute-start.1 = (f32[4,128,256]{2,1,0:T(8,128)}, f32[4,128,256]{2,1,0:T(8,128)}, u32[]{:S(2)}, u32[]{:S(2)}) collective-permute-start(f32[4,128,256]{2,1,0:T(8,128)} %bitcast.66), channel_id=1, source_target_pairs={{0,128},{128,0},{256,384},{384,256},{1,129},{129,1},{257,385},{385... | collective-permute-start | bytes 1572872 | tf_op jit(solution)/shard_map/ppermute | solution.py:66
  76.0 24.1 %all-to-all-start.2 = ((f32[4,128,256]{2,1,0:T(8,128)}), f32[4,128,256]{2,1,0:T(8,128)S(1)}, u32[]{:S(2)}, u32[]{:S(2)}) async-start(f32[4,128,256]{2,1,0:T(8,128)} %bitcast.68), calls=%async_computation.2 | async-start | bytes 1048576 | tf_op jit(solution)/shard_map/all_to_all | solution.py:69
  83.8 9.4 %collective-permute-start.4 = (f32[256,256]{1,0:T(8,128)S(1)}, f32[256,256]{1,0:T(8,128)S(1)}, u32[]{:S(2)}, u32[]{:S(2)}) collective-permute-start(f32[256,256]{1,0:T(8,128)S(1)} %pad_maximum_fusion.6), channel_id=1, source_target_pairs={{0,6},{2,0},{4,2},{6,4},{1,7},{3,1},{5,3},{7,5},{8,14},{10,8},{12,... | collective-permute-start | bytes 786440 | tf_op jit(solution)/shard_map/ppermute | solution.py:77
  88.0 8.9 %collective-permute-start.3 = (f32[256,256]{1,0:T(8,128)S(1)}, f32[256,256]{1,0:T(8,128)S(1)}, u32[]{:S(2)}, u32[]{:S(2)}) collective-permute-start(f32[256,256]{1,0:T(8,128)S(1)} %pad_maximum_fusion.5), channel_id=1, source_target_pairs={{0,4},{2,6},{4,0},{6,2},{1,5},{3,7},{5,1},{7,3},{8,12},{10,14},{12... | collective-permute-start | bytes 786440 | tf_op jit(solution)/shard_map/ppermute | solution.py:77
  90.5 9.2 %collective-permute-start.2 = (f32[256,256]{1,0:T(8,128)S(1)}, f32[256,256]{1,0:T(8,128)S(1)}, u32[]{:S(2)}, u32[]{:S(2)}) collective-permute-start(f32[256,256]{1,0:T(8,128)S(1)} %pad_maximum_fusion.4), channel_id=1, source_target_pairs={{0,2},{2,4},{4,6},{6,0},{1,3},{3,5},{5,7},{7,1},{8,10},{10,12},{12... | collective-permute-start | bytes 786440 | tf_op jit(solution)/shard_map/ppermute | solution.py:77
  114.0 34.9 %copy-start = (f32[8,2048]{1,0:T(8,128)S(1)}, f32[8,2048]{1,0:T(8,128)}, u32[]{:S(2)}) copy-start(f32[8,2048]{1,0:T(8,128)} %param.6) | copy-start | bytes 196612
  135.0 13.8 %all-to-all-start.4 = ((f32[8,8,1024]{2,1,0:T(8,128)}), f32[8,8,1024]{2,1,0:T(8,128)S(1)}, u32[]{:S(2)}, u32[]{:S(2)}) async-start(f32[8,8,1024]{2,1,0:T(8,128)} %bitcast.30), calls=%async_computation.4 | async-start | bytes 524288 | tf_op jit(solution)/shard_map/all_to_all | solution.py:90

commit v5 on v4

--- a/solution.py
+++ b/solution.py
@@ -44,33 +44,48 @@
     c = lax.axis_index("c")
 
     moved = lax.ppermute(panel, AXES, turn_pairs())
-    own = lax.dynamic_slice(
-        pattern, ((x * 4 + y) * 2 + c, (zl * 4 + zh) * 2), (1, 2)
-    ).astype(jnp.float32)
-    moved = moved * jnp.repeat(own, 128, axis=1)
+
+    def pattern_row(x):
+        row = lax.dynamic_slice_in_dim(pattern, (x * 4 + y) * 2 + c, 1, 0)
+        return row.astype(jnp.float32).reshape(4, 4, 2)
+
+    row, pair_row = pattern_row(x), pattern_row(x ^ 1)
+    mask = jnp.repeat(pick(row, zh, 1), 128, axis=1)[:, None, :]
+    masks = [jnp.repeat(pick(r, zl), 128, axis=1)[:, None, :] for r in (row, pair_row)]
 
     a_cols = lax.all_gather(ancestor_inverse, "c", axis=0)
     a_cols = jnp.concatenate([a_cols[0], a_cols[1]], axis=1)
-    a_copies, moved = lax.optimization_barrier((jnp.stack([a_cols] * 4), moved))
+    a_copies, moved, mask, masks = lax.optimization_barrier(
+        (jnp.stack([a_cols] * 4), moved, mask, masks)
+    )
     a_all = lax.all_to_all(a_copies, "x", 0, 0, tiled=True).reshape(1024, 256)
 
     over_zl = lax.all_gather(moved, "zl", axis=0)
     over_zl, a_all = lax.optimization_barrier((over_zl, a_all))
-    over_zl = over_zl.transpose(1, 0, 2).reshape(128, 1024)
+    over_zl = over_zl * mask
     copies = lax.optimization_barrier(jnp.stack([over_zl] * 4))
-    by_y = lax.all_to_all(copies, "y", 0, 0, tiled=True).reshape(512, 1024)
+    by_y = lax.all_to_all(copies, "y", 0, 0, tiled=True)
 
     moved, _ = lax.optimization_barrier((moved, copies))
     over_zh = lax.all_gather(moved, "zh", axis=0)
     by_y, over_zh = lax.optimization_barrier((by_y, over_zh))
     pair_zh = lax.ppermute(over_zh, "x", [(i, i ^ 1) for i in range(4)])
 
-    partial = dot(by_y, a_all, ((1,), (0,)))
+    partial = sum(
+        dot(
+            by_y[:, k].reshape(512, 256), a_all[256 * k : 256 * (k + 1)],
+            ((1,), (0,)),
+        )
+        for k in range(4)
+    )
     summed = lax.all_to_all(partial, "zh", 0, 0, tiled=True)
     summed = -jnp.sum(summed.reshape(4, 128, 256), axis=0)
 
     def column(index):
-        return jnp.concatenate([pick(over_zh, index), pick(pair_zh, index)])
+        pair = (over_zh, pair_zh)
+        return jnp.concatenate(
+            [pick(b, index) * pick(m, index) for b, m in zip(pair, masks)]
+        )
 
     over_zh, pair_zh, _ = lax.optimization_barrier((over_zh, pair_zh, partial))
     pieces = [column(y)] + [

time: 150 us -> 150 us (level)
  transfers between devices with their start and end apart: 9 -> 9, of which waited for: 3 -> 3; matrix products, arithmetic and copies ran while one was open for 3% -> 4% of each run, Pallas kernels for 0% -> 0%
where the time goes in v5:
time: 150 us
  blocking collectives  87.1 us (58%)
  starting transfers between devices  36.2 us (24%)
  waiting for transfers between devices  14.7 us (10%)
  local copies, waits for them, and re-layouts  4.04 us (3%)
  other arithmetic  3.75 us (2%)
  matrix products  2.94 us (2%)
    all_gather x1, blocking collectives, on_device(): over_zh = lax.all_gather(moved, 'zh', axis=0)  31 us
    all_to_all x1, blocking collectives, on_device(): over_y = lax.all_to_all(coupling, 'y', 0, 0, tiled=True)  19.5 us
    all_gather x1, blocking collectives, on_device(): rows = lax.all_gather(summed, 'c', axis=0, tiled=True)  14 us
    all_gather x1, blocking collectives, on_device(): over_zl = lax.all_gather(moved, 'zl', axis=0)  13.9 us
    ppermute x3, starting transfers between devices, on_device(): lax.ppermute(column((y + s) % 4), 'y', shift_pairs(s))  9.19 us
    all_gather x1, blocking collectives, on_device(): a_cols = lax.all_gather(ancestor_inverse, 'c', axis=0)  8.71 us
    all_to_all x1, waiting for transfers between devices, on_device(): over_l = lax.all_to_all(sum_y, ('zl', 'c'), 0, 0, tiled=True)  8.06 us
    ppermute x3, waiting for transfers between devices, on_device(): lax.ppermute(column((y + s) % 4), 'y', shift_pairs(s))  6.6 us
  transfers between devices with their start and end apart: 9, of which 3 were waited for; matrix products, arithmetic and copies ran while one was open for 4% of the time, Pallas kernels for 0%

profile of v5, /device:TPU:1, one launch (start us, length us, event | category | flops | bytes accessed | tf_op | source)
XLA Modules:
  0.0 149.7 jit_solution(15268978575909547726)
XLA Ops:
  0.6 1.6 %collective-permute-start = (f32[128,256]{1,0:T(8,128)}, f32[128,256]{1,0:T(8,128)S(1)}, u32[]{:S(2)}, u32[]{:S(2)}) collective-permute-start(f32[128,256]{1,0:T(8,128)} %param.4), channel_id=1, source_target_pairs={{0,0},{1,1},{2,2},{3,3},{4,4},{5,5},{6,6},{7,7},{8,128},{9,129},{1... | collective-permute-start | bytes 393224 | tf_op jit(solution)/shard_map/ppermute | solution.py:46
  2.2 8.7 %all-gather = f32[512,128]{1,0:T(8,128)S(1)} all-gather(f32[256,128]{1,0:T(8,128)} %param.5), channel_id=2, replica_groups=mesh['x'=4,'zh'=4,'zl'=4,'y'=4,'c'=2] {'c'}, dimensions={0}, use_global_device_ids=true | all-gather | bytes 393216 | tf_op jit(solution)/shard_map/all_gather | solution.py:56
  10.9 0.7 fusion.10
  12.2 1.0 stack.53
  13.2 6.3 %all-to-all-start = ((f32[4,256,256]{2,1,0:T(8,128)}), f32[4,256,256]{2,1,0:T(8,128)S(1)}, u32[]{:S(2)}, u32[]{:S(2)}) async-start(f32[4,256,256]{2,1,0:T(8,128)} %stack.53), calls=%async_computation | async-start | bytes 2097152 | tf_op jit(solution)/shard_map/all_to_all | solution.py:61
  19.5 13.9 %all-gather.1 = f32[512,256]{1,0:T(8,128)S(1)} all-gather(f32[128,256]{1,0:T(8,128)S(1)} %collective-permute-done), channel_id=3, replica_groups=mesh['x'=4,'zh'=4,'zl'=4,'y'=4,'c'=2] {'zl'}, dimensions={0}, use_global_device_ids=true | all-gather | bytes 655360 | tf_op jit(solution)/shard_map/all_gather | solution.py:63
  33.5 1.5 %stack.54 = f32[4,4,128,256]{3,2,1,0:T(8,128)} broadcast(f32[4,128,256]{2,1,0:T(8,128)S(1)} %broadcast_multiply_fusion), dimensions={1,2,3} | broadcast | bytes 2621440 | tf_op jit(solution)/shard_map/stack | solution.py:66
  35.0 4.2 %all-to-all-start.1 = ((f32[4,4,128,256]{3,2,1,0:T(8,128)}), f32[4,4,128,256]{3,2,1,0:T(8,128)S(1)}, u32[]{:S(2)}, u32[]{:S(2)}) async-start(f32[4,4,128,256]{3,2,1,0:T(8,128)} %stack.54), calls=%async_computation.1 | async-start | bytes 4194304 | tf_op jit(solution)/shard_map/all_to_all | solution.py:67
  39.2 31.0 %all-gather.2 = f32[512,256]{1,0:T(8,128)} all-gather(f32[128,256]{1,0:T(8,128)S(1)} %collective-permute-done), channel_id=4, replica_groups=mesh['x'=4,'zh'=4,'zl'=4,'y'=4,'c'=2] {'zh'}, dimensions={0}, use_global_device_ids=true | all-gather | bytes 655360 | tf_op jit(solution)/shard_map/all_gather | solution.py:70
  70.2 0.1 fusion.11
  70.4 3.5 %collective-permute-start.1 = (f32[4,128,256]{2,1,0:T(8,128)}, f32[4,128,256]{2,1,0:T(8,128)S(1)}, u32[]{:S(2)}, u32[]{:S(2)}) collective-permute-start(f32[4,128,256]{2,1,0:T(8,128)} %bitcast.6), channel_id=1, source_target_pairs={{0,128},{128,0},{256,384},{384,256},{1,129},{129,1},{257,385},{385... | collective-permute-start | bytes 1572872 | tf_op jit(solution)/shard_map/ppermute | solution.py:72
  73.9 0.4 fusion.3
  74.3 0.4 convolution_add_fusion.2
  74.7 0.4 convolution_add_fusion.1
  75.1 1.2 convolution_add_fusion
  76.2 6.4 %all-to-all-start.2 = ((f32[4,128,256]{2,1,0:T(8,128)}), f32[4,128,256]{2,1,0:T(8,128)S(1)}, u32[]{:S(2)}, u32[]{:S(2)}) async-start(f32[4,128,256]{2,1,0:T(8,128)} %bitcast.11), calls=%async_computation.2 | async-start | bytes 1048576 | tf_op jit(solution)/shard_map/all_to_all | solution.py:81
  82.7 1.1 bitcast_multiply_fusion.7
  83.9 4.2 %collective-permute-start.4 = (f32[256,256]{1,0:T(8,128)S(1)}, f32[256,256]{1,0:T(8,128)S(1)}, u32[]{:S(2)}, u32[]{:S(2)}) collective-permute-start(f32[256,256]{1,0:T(8,128)S(1)} %pad_maximum_fusion.6), channel_id=1, source_target_pairs={{0,6},{2,0},{4,2},{6,4},{1,7},{3,1},{5,3},{7,5},{8,14},{10,8},{12,... | collective-permute-start | bytes 786440 | tf_op jit(solution)/shard_map/ppermute | solution.py:92
  88.1 2.5 %collective-permute-start.3 = (f32[256,256]{1,0:T(8,128)S(1)}, f32[256,256]{1,0:T(8,128)S(1)}, u32[]{:S(2)}, u32[]{:S(2)}) collective-permute-start(f32[256,256]{1,0:T(8,128)S(1)} %pad_maximum_fusion.5), channel_id=1, source_target_pairs={{0,4},{2,6},{4,0},{6,2},{1,5},{3,7},{5,1},{7,3},{8,12},{10,14},{12... | collective-permute-start | bytes 786440 | tf_op jit(solution)/shard_map/ppermute | solution.py:92
  90.7 2.5 %collective-permute-start.2 = (f32[256,256]{1,0:T(8,128)S(1)}, f32[256,256]{1,0:T(8,128)S(1)}, u32[]{:S(2)}, u32[]{:S(2)}) collective-permute-start(f32[256,256]{1,0:T(8,128)S(1)} %pad_maximum_fusion.4), channel_id=1, source_target_pairs={{0,2},{2,4},{4,6},{6,0},{1,3},{3,5},{5,7},{7,1},{8,10},{10,12},{12... | collective-permute-start | bytes 786440 | tf_op jit(solution)/shard_map/ppermute | solution.py:92
  93.3 3.8 %collective-permute-done.3 = f32[256,256]{1,0:T(8,128)S(1)} collective-permute-done((f32[256,256]{1,0:T(8,128)S(1)}, f32[256,256]{1,0:T(8,128)S(1)}, u32[]{:S(2)}, u32[]{:S(2)}) %collective-permute-start.3) | collective-permute-done | bytes 262176 | tf_op jit(solution)/shard_map/ppermute | solution.py:92
  97.0 2.8 %collective-permute-done.2 = f32[256,256]{1,0:T(8,128)S(1)} collective-permute-done((f32[256,256]{1,0:T(8,128)S(1)}, f32[256,256]{1,0:T(8,128)S(1)}, u32[]{:S(2)}, u32[]{:S(2)}) %collective-permute-start.2) | collective-permute-done | bytes 262176 | tf_op jit(solution)/shard_map/ppermute | solution.py:92
  99.9 0.1 pad_maximum_fusion
  100.1 0.1 pad_maximum_fusion.1
  100.2 14.0 %all_gather.27 = f32[256,256]{1,0:T(8,128)S(1)} all-gather(f32[128,256]{1,0:T(8,128)S(1)} %neg.3), channel_id=1, replica_groups=mesh['x'=4,'zh'=4,'zl'=4,'y'=4,'c'=2] {'c'}, dimensions={0}, use_global_device_ids=true | all-gather | bytes 393216 | tf_op jit(solution)/shard_map/all_gather | solution.py:98
  114.3 0.6 fusion.13
  114.9 19.5 %all_to_all.34 = f32[4,64,1024]{2,1,0:T(8,128)S(1)} all-to-all(f32[4,64,1024]{2,1,0:T(8,128)S(1)} %fusion.13), channel_id=1, replica_groups=mesh['x'=4,'zh'=4,'zl'=4,'y'=4,'c'=2] {'y'}, dimensions={0} | all-to-all | bytes 2097152 | tf_op jit(solution)/shard_map/all_to_all | solution.py:103
  134.4 0.8 reduce_sum.28
  135.2 5.1 %all-to-all-start.4 = ((f32[8,8,1024]{2,1,0:T(8,128)}), f32[8,8,1024]{2,1,0:T(8,128)S(1)}, u32[]{:S(2)}, u32[]{:S(2)}) async-start(f32[8,8,1024]{2,1,0:T(8,128)} %bitcast.41), calls=%async_computation.4 | async-start | bytes 524288 | tf_op jit(solution)/shard_map/all_to_all | solution.py:105
  140.3 0.7 constant_dynamic-slice_fusion.8
  140.9 8.1 %all-to-all-done.4 = f32[8,8,1024]{2,1,0:T(8,128)S(1)} async-done(((f32[8,8,1024]{2,1,0:T(8,128)}), f32[8,8,1024]{2,1,0:T(8,128)S(1)}, u32[]{:S(2)}, u32[]{:S(2)}) %all-to-all-start.4) | async-done | bytes 262176 | tf_op jit(solution)/shard_map/all_to_all | solution.py:105
  149.1 0.6 sub.15
  (36 shorter events, 0.9 us)
Async XLA Ops:
  0.6 11.6 %collective-permute-start = (f32[128,256]{1,0:T(8,128)}, f32[128,256]{1,0:T(8,128)S(1)}, u32[]{:S(2)}, u32[]{:S(2)}) collective-permute-start(f32[128,256]{1,0:T(8,128)} %param.4), channel_id=1, source_target_pairs={{0,0},{1,1},{2,2},{3,3},{4,4},{5,5},{6,6},{7,7},{8,128},{9,129},{1... | collective-permute-start | bytes 393224 | tf_op jit(solution)/shard_map/ppermute | solution.py:46
  13.2 20.2 %all-to-all-start = ((f32[4,256,256]{2,1,0:T(8,128)}), f32[4,256,256]{2,1,0:T(8,128)S(1)}, u32[]{:S(2)}, u32[]{:S(2)}) async-start(f32[4,256,256]{2,1,0:T(8,128)} %stack.53), calls=%async_computation | async-start | bytes 2097152 | tf_op jit(solution)/shard_map/all_to_all | solution.py:61
  35.0 35.2 %all-to-all-start.1 = ((f32[4,4,128,256]{3,2,1,0:T(8,128)}), f32[4,4,128,256]{3,2,1,0:T(8,128)S(1)}, u32[]{:S(2)}, u32[]{:S(2)}) async-start(f32[4,4,128,256]{3,2,1,0:T(8,128)} %stack.54), calls=%async_computation.1 | async-start | bytes 4194304 | tf_op jit(solution)/shard_map/all_to_all | solution.py:67
  70.4 12.2 %collective-permute-start.1 = (f32[4,128,256]{2,1,0:T(8,128)}, f32[4,128,256]{2,1,0:T(8,128)S(1)}, u32[]{:S(2)}, u32[]{:S(2)}) collective-permute-start(f32[4,128,256]{2,1,0:T(8,128)} %bitcast.6), channel_id=1, source_target_pairs={{0,128},{128,0},{256,384},{384,256},{1,129},{129,1},{257,385},{385... | collective-permute-start | bytes 1572872 | tf_op jit(solution)/shard_map/ppermute | solution.py:72
  76.2 23.9 %all-to-all-start.2 = ((f32[4,128,256]{2,1,0:T(8,128)}), f32[4,128,256]{2,1,0:T(8,128)S(1)}, u32[]{:S(2)}, u32[]{:S(2)}) async-start(f32[4,128,256]{2,1,0:T(8,128)} %bitcast.11), calls=%async_computation.2 | async-start | bytes 1048576 | tf_op jit(solution)/shard_map/all_to_all | solution.py:81
  83.9 9.4 %collective-permute-start.4 = (f32[256,256]{1,0:T(8,128)S(1)}, f32[256,256]{1,0:T(8,128)S(1)}, u32[]{:S(2)}, u32[]{:S(2)}) collective-permute-start(f32[256,256]{1,0:T(8,128)S(1)} %pad_maximum_fusion.6), channel_id=1, source_target_pairs={{0,6},{2,0},{4,2},{6,4},{1,7},{3,1},{5,3},{7,5},{8,14},{10,8},{12,... | collective-permute-start | bytes 786440 | tf_op jit(solution)/shard_map/ppermute | solution.py:92
  88.1 8.9 %collective-permute-start.3 = (f32[256,256]{1,0:T(8,128)S(1)}, f32[256,256]{1,0:T(8,128)S(1)}, u32[]{:S(2)}, u32[]{:S(2)}) collective-permute-start(f32[256,256]{1,0:T(8,128)S(1)} %pad_maximum_fusion.5), channel_id=1, source_target_pairs={{0,4},{2,6},{4,0},{6,2},{1,5},{3,7},{5,1},{7,3},{8,12},{10,14},{12... | collective-permute-start | bytes 786440 | tf_op jit(solution)/shard_map/ppermute | solution.py:92
  90.7 9.2 %collective-permute-start.2 = (f32[256,256]{1,0:T(8,128)S(1)}, f32[256,256]{1,0:T(8,128)S(1)}, u32[]{:S(2)}, u32[]{:S(2)}) collective-permute-start(f32[256,256]{1,0:T(8,128)S(1)} %pad_maximum_fusion.4), channel_id=1, source_target_pairs={{0,2},{2,4},{4,6},{6,0},{1,3},{3,5},{5,7},{7,1},{8,10},{10,12},{12... | collective-permute-start | bytes 786440 | tf_op jit(solution)/shard_map/ppermute | solution.py:92
  114.9 34.2 %copy-start = (f32[8,2048]{1,0:T(8,128)S(1)}, f32[8,2048]{1,0:T(8,128)}, u32[]{:S(2)}) copy-start(f32[8,2048]{1,0:T(8,128)} %param.6) | copy-start | bytes 196612
  135.2 13.8 %all-to-all-start.4 = ((f32[8,8,1024]{2,1,0:T(8,128)}), f32[8,8,1024]{2,1,0:T(8,128)S(1)}, u32[]{:S(2)}, u32[]{:S(2)}) async-start(f32[8,8,1024]{2,1,0:T(8,128)} %bitcast.41), calls=%async_computation.4 | async-start | bytes 524288 | tf_op jit(solution)/shard_map/all_to_all | solution.py:105

commit v6 on v5

--- a/solution.py
+++ b/solution.py
@@ -98,11 +98,12 @@
     rows = lax.all_gather(summed, "c", axis=0, tiled=True)
     inverse_rows = lax.dynamic_slice_in_dim(rows, c * 128, 128, 1)
 
-    lhs = rows.reshape(4, 4, 16, 256).transpose(1, 0, 2, 3).reshape(256, 256)
-    coupling = dot(lhs, col_form, ((1,), (1,)))
-    over_y = lax.all_to_all(coupling, "y", 0, 0, tiled=True)
-    sum_y = jnp.sum(over_y.reshape(4, 64, 1024), axis=0)
-    over_l = lax.all_to_all(sum_y, ("zl", "c"), 0, 0, tiled=True)
+    lhs = rows.reshape(4, 4, 2, 8, 256).transpose(1, 2, 0, 3, 4)
+    coupling = dot(lhs.reshape(256, 256), col_form, ((1,), (1,)))
+    over_y = lax.all_to_all(coupling, ("y", "c"), 0, 0, tiled=True)
+    sum_y = jnp.sum(over_y.reshape(4, 2, 4, 8, 1024), axis=0)
+    sum_y = sum_y.transpose(1, 0, 2, 3).reshape(64, 1024)
+    over_l = lax.all_to_all(sum_y, "zl", 0, 0, tiled=True)
     both = jnp.sum(over_l.reshape(4, 2, 8, 2, 4, 128), axis=0)
     both = both.transpose(2, 1, 3, 0, 4)
     both = jnp.stack([pick(both, (b + x) % 2) for b in range(2)], axis=1)

time: 150 us -> 150 us (level); the launches traced: 150 us -> 148 us
  starting transfers between devices: 36.2 us -> 34.5 us
    all_to_all x1, starting transfers between devices: 5.11 us -> 3.4 us  [on_device(): over_l = lax.all_to_all(sum_y, 'zl', 0, 0, tiled=True)]
where the time goes in v6:
time: 150 us; the launch traced here: 148 us
  blocking collectives  88.4 us (59%)
  starting transfers between devices  34.5 us (23%)
  waiting for transfers between devices  13.5 us (9%)
  local copies, waits for them, and re-layouts  4.76 us (3%)
  other arithmetic  3.05 us (2%)
  matrix products  2.94 us (2%)
    all_gather x1, blocking collectives, on_device(): over_zh = lax.all_gather(moved, 'zh', axis=0)  31 us
    all_to_all x1, blocking collectives, on_device(): over_y = lax.all_to_all(coupling, ('y', 'c'), 0, 0, tiled=True)  20.8 us
    all_gather x1, blocking collectives, on_device(): rows = lax.all_gather(summed, 'c', axis=0, tiled=True)  14 us
    all_gather x1, blocking collectives, on_device(): over_zl = lax.all_gather(moved, 'zl', axis=0)  13.9 us
    ppermute x3, starting transfers between devices, on_device(): lax.ppermute(column((y + s) % 4), 'y', shift_pairs(s))  9.19 us
    all_gather x1, blocking collectives, on_device(): a_cols = lax.all_gather(ancestor_inverse, 'c', axis=0)  8.71 us
    all_to_all x1, waiting for transfers between devices, on_device(): over_l = lax.all_to_all(sum_y, 'zl', 0, 0, tiled=True)  6.84 us
    ppermute x3, waiting for transfers between devices, on_device(): lax.ppermute(column((y + s) % 4), 'y', shift_pairs(s))  6.6 us
  transfers between devices with their start and end apart: 9, of which 3 were waited for; matrix products, arithmetic and copies ran while one was open for 4% of the time, Pallas kernels for 0%

profile of v6, /device:TPU:1, one launch (start us, length us, event | category | flops | bytes accessed | tf_op | source)
XLA Modules:
  0.0 148.2 jit_solution(1750779593780236209)
XLA Ops:
  0.6 1.6 %collective-permute-start = (f32[128,256]{1,0:T(8,128)}, f32[128,256]{1,0:T(8,128)S(1)}, u32[]{:S(2)}, u32[]{:S(2)}) collective-permute-start(f32[128,256]{1,0:T(8,128)} %param.4), channel_id=1, source_target_pairs={{0,0},{1,1},{2,2},{3,3},{4,4},{5,5},{6,6},{7,7},{8,128},{9,129},{1... | collective-permute-start | bytes 393224 | tf_op jit(solution)/shard_map/ppermute | solution.py:46
  2.2 8.7 %all-gather = f32[512,128]{1,0:T(8,128)S(1)} all-gather(f32[256,128]{1,0:T(8,128)} %param.5), channel_id=2, replica_groups=mesh['x'=4,'zh'=4,'zl'=4,'y'=4,'c'=2] {'c'}, dimensions={0}, use_global_device_ids=true | all-gather | bytes 393216 | tf_op jit(solution)/shard_map/all_gather | solution.py:56
  10.9 0.7 fusion.10
  12.2 1.0 stack.53
  13.2 6.3 %all-to-all-start = ((f32[4,256,256]{2,1,0:T(8,128)}), f32[4,256,256]{2,1,0:T(8,128)S(1)}, u32[]{:S(2)}, u32[]{:S(2)}) async-start(f32[4,256,256]{2,1,0:T(8,128)} %stack.53), calls=%async_computation | async-start | bytes 2097152 | tf_op jit(solution)/shard_map/all_to_all | solution.py:61
  19.5 13.9 %all-gather.1 = f32[512,256]{1,0:T(8,128)S(1)} all-gather(f32[128,256]{1,0:T(8,128)S(1)} %collective-permute-done), channel_id=3, replica_groups=mesh['x'=4,'zh'=4,'zl'=4,'y'=4,'c'=2] {'zl'}, dimensions={0}, use_global_device_ids=true | all-gather | bytes 655360 | tf_op jit(solution)/shard_map/all_gather | solution.py:63
  33.5 1.5 %stack.54 = f32[4,4,128,256]{3,2,1,0:T(8,128)} broadcast(f32[4,128,256]{2,1,0:T(8,128)S(1)} %broadcast_multiply_fusion), dimensions={1,2,3} | broadcast | bytes 2621440 | tf_op jit(solution)/shard_map/stack | solution.py:66
  35.0 4.2 %all-to-all-start.1 = ((f32[4,4,128,256]{3,2,1,0:T(8,128)}), f32[4,4,128,256]{3,2,1,0:T(8,128)S(1)}, u32[]{:S(2)}, u32[]{:S(2)}) async-start(f32[4,4,128,256]{3,2,1,0:T(8,128)} %stack.54), calls=%async_computation.1 | async-start | bytes 4194304 | tf_op jit(solution)/shard_map/all_to_all | solution.py:67
  39.2 31.0 %all-gather.2 = f32[512,256]{1,0:T(8,128)} all-gather(f32[128,256]{1,0:T(8,128)S(1)} %collective-permute-done), channel_id=4, replica_groups=mesh['x'=4,'zh'=4,'zl'=4,'y'=4,'c'=2] {'zh'}, dimensions={0}, use_global_device_ids=true | all-gather | bytes 655360 | tf_op jit(solution)/shard_map/all_gather | solution.py:70
  70.2 0.1 fusion.11
  70.4 3.5 %collective-permute-start.1 = (f32[4,128,256]{2,1,0:T(8,128)}, f32[4,128,256]{2,1,0:T(8,128)S(1)}, u32[]{:S(2)}, u32[]{:S(2)}) collective-permute-start(f32[4,128,256]{2,1,0:T(8,128)} %bitcast.6), channel_id=1, source_target_pairs={{0,128},{128,0},{256,384},{384,256},{1,129},{129,1},{257,385},{385... | collective-permute-start | bytes 1572872 | tf_op jit(solution)/shard_map/ppermute | solution.py:72
  73.9 0.4 fusion.3
  74.3 0.4 convolution_add_fusion.2
  74.7 0.4 convolution_add_fusion.1
  75.1 1.2 convolution_add_fusion
  76.2 6.4 %all-to-all-start.2 = ((f32[4,128,256]{2,1,0:T(8,128)}), f32[4,128,256]{2,1,0:T(8,128)S(1)}, u32[]{:S(2)}, u32[]{:S(2)}) async-start(f32[4,128,256]{2,1,0:T(8,128)} %bitcast.11), calls=%async_computation.2 | async-start | bytes 1048576 | tf_op jit(solution)/shard_map/all_to_all | solution.py:81
  82.7 1.1 bitcast_multiply_fusion.7
  83.9 4.2 %collective-permute-start.4 = (f32[256,256]{1,0:T(8,128)S(1)}, f32[256,256]{1,0:T(8,128)S(1)}, u32[]{:S(2)}, u32[]{:S(2)}) collective-permute-start(f32[256,256]{1,0:T(8,128)S(1)} %pad_maximum_fusion.6), channel_id=1, source_target_pairs={{0,6},{2,0},{4,2},{6,4},{1,7},{3,1},{5,3},{7,5},{8,14},{10,8},{12,... | collective-permute-start | bytes 786440 | tf_op jit(solution)/shard_map/ppermute | solution.py:92
  88.1 2.5 %collective-permute-start.3 = (f32[256,256]{1,0:T(8,128)S(1)}, f32[256,256]{1,0:T(8,128)S(1)}, u32[]{:S(2)}, u32[]{:S(2)}) collective-permute-start(f32[256,256]{1,0:T(8,128)S(1)} %pad_maximum_fusion.5), channel_id=1, source_target_pairs={{0,4},{2,6},{4,0},{6,2},{1,5},{3,7},{5,1},{7,3},{8,12},{10,14},{12... | collective-permute-start | bytes 786440 | tf_op jit(solution)/shard_map/ppermute | solution.py:92
  90.7 2.5 %collective-permute-start.2 = (f32[256,256]{1,0:T(8,128)S(1)}, f32[256,256]{1,0:T(8,128)S(1)}, u32[]{:S(2)}, u32[]{:S(2)}) collective-permute-start(f32[256,256]{1,0:T(8,128)S(1)} %pad_maximum_fusion.4), channel_id=1, source_target_pairs={{0,2},{2,4},{4,6},{6,0},{1,3},{3,5},{5,7},{7,1},{8,10},{10,12},{12... | collective-permute-start | bytes 786440 | tf_op jit(solution)/shard_map/ppermute | solution.py:92
  93.3 3.8 %collective-permute-done.3 = f32[256,256]{1,0:T(8,128)S(1)} collective-permute-done((f32[256,256]{1,0:T(8,128)S(1)}, f32[256,256]{1,0:T(8,128)S(1)}, u32[]{:S(2)}, u32[]{:S(2)}) %collective-permute-start.3) | collective-permute-done | bytes 262176 | tf_op jit(solution)/shard_map/ppermute | solution.py:92
  97.0 2.8 %collective-permute-done.2 = f32[256,256]{1,0:T(8,128)S(1)} collective-permute-done((f32[256,256]{1,0:T(8,128)S(1)}, f32[256,256]{1,0:T(8,128)S(1)}, u32[]{:S(2)}, u32[]{:S(2)}) %collective-permute-start.2) | collective-permute-done | bytes 262176 | tf_op jit(solution)/shard_map/ppermute | solution.py:92
  99.9 0.1 pad_maximum_fusion
  100.1 0.1 pad_maximum_fusion.1
  100.2 14.0 %all_gather.27 = f32[256,256]{1,0:T(8,128)S(1)} all-gather(f32[128,256]{1,0:T(8,128)S(1)} %neg.3), channel_id=1, replica_groups=mesh['x'=4,'zh'=4,'zl'=4,'y'=4,'c'=2] {'c'}, dimensions={0}, use_global_device_ids=true | all-gather | bytes 393216 | tf_op jit(solution)/shard_map/all_gather | solution.py:98
  114.3 0.6 fusion.13
  114.9 20.8 %all_to_all.34 = f32[8,32,1024]{2,1,0:T(8,128)S(1)} all-to-all(f32[8,32,1024]{2,1,0:T(8,128)S(1)} %fusion.13), channel_id=1, replica_groups=mesh['x'=4,'zh'=4,'zl'=4,'y'=4,'c'=2] {'y','c'}, dimensions={0} | all-to-all | bytes 2097152 | tf_op jit(solution)/shard_map/all_to_all | solution.py:103
  135.8 0.7 copy_bitcast_fusion
  136.5 3.4 %all-to-all-start.4 = ((f32[4,16,1024]{2,1,0:T(8,128)}), f32[4,16,1024]{2,1,0:T(8,128)S(1)}, u32[]{:S(2)}, u32[]{:S(2)}) async-start(f32[4,16,1024]{2,1,0:T(8,128)} %copy_bitcast_fusion), calls=%async_computation.4 | async-start | bytes 524288 | tf_op jit(solution)/shard_map/all_to_all | solution.py:106
  139.9 0.7 constant_dynamic-slice_fusion.8
  140.6 6.8 %all-to-all-done.4 = f32[4,16,1024]{2,1,0:T(8,128)S(1)} async-done(((f32[4,16,1024]{2,1,0:T(8,128)}), f32[4,16,1024]{2,1,0:T(8,128)S(1)}, u32[]{:S(2)}, u32[]{:S(2)}) %all-to-all-start.4) | async-done | bytes 262176 | tf_op jit(solution)/shard_map/all_to_all | solution.py:106
  147.5 0.6 sub.15
  (37 shorter events, 1.0 us)
Async XLA Ops:
  0.6 11.6 %collective-permute-start = (f32[128,256]{1,0:T(8,128)}, f32[128,256]{1,0:T(8,128)S(1)}, u32[]{:S(2)}, u32[]{:S(2)}) collective-permute-start(f32[128,256]{1,0:T(8,128)} %param.4), channel_id=1, source_target_pairs={{0,0},{1,1},{2,2},{3,3},{4,4},{5,5},{6,6},{7,7},{8,128},{9,129},{1... | collective-permute-start | bytes 393224 | tf_op jit(solution)/shard_map/ppermute | solution.py:46
  13.2 20.2 %all-to-all-start = ((f32[4,256,256]{2,1,0:T(8,128)}), f32[4,256,256]{2,1,0:T(8,128)S(1)}, u32[]{:S(2)}, u32[]{:S(2)}) async-start(f32[4,256,256]{2,1,0:T(8,128)} %stack.53), calls=%async_computation | async-start | bytes 2097152 | tf_op jit(solution)/shard_map/all_to_all | solution.py:61
  35.0 35.2 %all-to-all-start.1 = ((f32[4,4,128,256]{3,2,1,0:T(8,128)}), f32[4,4,128,256]{3,2,1,0:T(8,128)S(1)}, u32[]{:S(2)}, u32[]{:S(2)}) async-start(f32[4,4,128,256]{3,2,1,0:T(8,128)} %stack.54), calls=%async_computation.1 | async-start | bytes 4194304 | tf_op jit(solution)/shard_map/all_to_all | solution.py:67
  70.4 12.2 %collective-permute-start.1 = (f32[4,128,256]{2,1,0:T(8,128)}, f32[4,128,256]{2,1,0:T(8,128)S(1)}, u32[]{:S(2)}, u32[]{:S(2)}) collective-permute-start(f32[4,128,256]{2,1,0:T(8,128)} %bitcast.6), channel_id=1, source_target_pairs={{0,128},{128,0},{256,384},{384,256},{1,129},{129,1},{257,385},{385... | collective-permute-start | bytes 1572872 | tf_op jit(solution)/shard_map/ppermute | solution.py:72
  76.2 23.9 %all-to-all-start.2 = ((f32[4,128,256]{2,1,0:T(8,128)}), f32[4,128,256]{2,1,0:T(8,128)S(1)}, u32[]{:S(2)}, u32[]{:S(2)}) async-start(f32[4,128,256]{2,1,0:T(8,128)} %bitcast.11), calls=%async_computation.2 | async-start | bytes 1048576 | tf_op jit(solution)/shard_map/all_to_all | solution.py:81
  83.9 9.4 %collective-permute-start.4 = (f32[256,256]{1,0:T(8,128)S(1)}, f32[256,256]{1,0:T(8,128)S(1)}, u32[]{:S(2)}, u32[]{:S(2)}) collective-permute-start(f32[256,256]{1,0:T(8,128)S(1)} %pad_maximum_fusion.6), channel_id=1, source_target_pairs={{0,6},{2,0},{4,2},{6,4},{1,7},{3,1},{5,3},{7,5},{8,14},{10,8},{12,... | collective-permute-start | bytes 786440 | tf_op jit(solution)/shard_map/ppermute | solution.py:92
  88.1 8.9 %collective-permute-start.3 = (f32[256,256]{1,0:T(8,128)S(1)}, f32[256,256]{1,0:T(8,128)S(1)}, u32[]{:S(2)}, u32[]{:S(2)}) collective-permute-start(f32[256,256]{1,0:T(8,128)S(1)} %pad_maximum_fusion.5), channel_id=1, source_target_pairs={{0,4},{2,6},{4,0},{6,2},{1,5},{3,7},{5,1},{7,3},{8,12},{10,14},{12... | collective-permute-start | bytes 786440 | tf_op jit(solution)/shard_map/ppermute | solution.py:92
  90.7 9.2 %collective-permute-start.2 = (f32[256,256]{1,0:T(8,128)S(1)}, f32[256,256]{1,0:T(8,128)S(1)}, u32[]{:S(2)}, u32[]{:S(2)}) collective-permute-start(f32[256,256]{1,0:T(8,128)S(1)} %pad_maximum_fusion.4), channel_id=1, source_target_pairs={{0,2},{2,4},{4,6},{6,0},{1,3},{3,5},{5,7},{7,1},{8,10},{10,12},{12... | collective-permute-start | bytes 786440 | tf_op jit(solution)/shard_map/ppermute | solution.py:92
  135.7 11.8 %copy-start = (f32[8,2048]{1,0:T(8,128)S(1)}, f32[8,2048]{1,0:T(8,128)}, u32[]{:S(2)}) copy-start(f32[8,2048]{1,0:T(8,128)} %param.6) | copy-start | bytes 196612
  136.5 10.9 %all-to-all-start.4 = ((f32[4,16,1024]{2,1,0:T(8,128)}), f32[4,16,1024]{2,1,0:T(8,128)S(1)}, u32[]{:S(2)}, u32[]{:S(2)}) async-start(f32[4,16,1024]{2,1,0:T(8,128)} %copy_bitcast_fusion), calls=%async_computation.4 | async-start | bytes 524288 | tf_op jit(solution)/shard_map/all_to_all | solution.py:106

commit v7 on v6

--- a/solution.py
+++ b/solution.py
@@ -88,10 +88,10 @@
         )
 
     over_zh, pair_zh, _ = lax.optimization_barrier((over_zh, pair_zh, partial))
-    pieces = [column(y)] + [
-        lax.ppermute(column((y + s) % 4), "y", shift_pairs(s)) for s in (1, 2, 3)
+    two, one, three = [
+        lax.ppermute(column((y + s) % 4), "y", shift_pairs(s)) for s in (2, 1, 3)
     ]
-    pieces = jnp.stack(pieces).reshape(4, 2, 128, 256)
+    pieces = jnp.stack([column(y), one, two, three]).reshape(4, 2, 128, 256)
     col_form = jnp.stack([pick(pieces, (y - b) % 4) for b in range(4)], axis=1)
     col_form = col_form.reshape(1024, 256)
 

time: 150 us -> 150 us (level)
  no operation moved by 1% of the time
where the time goes in v7:
time: 150 us; the launch traced here: 148 us
  blocking collectives  88.4 us (59%)
  starting transfers between devices  34.5 us (23%)
  waiting for transfers between devices  13.5 us (9%)
  local copies, waits for them, and re-layouts  4.76 us (3%)
  other arithmetic  3.05 us (2%)
  matrix products  2.94 us (2%)
    all_gather x1, blocking collectives, on_device(): over_zh = lax.all_gather(moved, 'zh', axis=0)  31 us
    all_to_all x1, blocking collectives, on_device(): over_y = lax.all_to_all(coupling, ('y', 'c'), 0, 0, tiled=True)  20.8 us
    all_gather x1, blocking collectives, on_device(): rows = lax.all_gather(summed, 'c', axis=0, tiled=True)  14 us
    all_gather x1, blocking collectives, on_device(): over_zl = lax.all_gather(moved, 'zl', axis=0)  13.9 us
    ppermute x3, starting transfers between devices, on_device(): lax.ppermute(column((y + s) % 4), 'y', shift_pairs(s))  9.19 us
    all_gather x1, blocking collectives, on_device(): a_cols = lax.all_gather(ancestor_inverse, 'c', axis=0)  8.71 us
    all_to_all x1, waiting for transfers between devices, on_device(): over_l = lax.all_to_all(sum_y, 'zl', 0, 0, tiled=True)  6.84 us
    ppermute x3, waiting for transfers between devices, on_device(): lax.ppermute(column((y + s) % 4), 'y', shift_pairs(s))  6.6 us
  transfers between devices with their start and end apart: 9, of which 3 were waited for; matrix products, arithmetic and copies ran while one was open for 4% of the time, Pallas kernels for 0%

profile of v7, /device:TPU:1, one launch (start us, length us, event | category | flops | bytes accessed | tf_op | source)
XLA Modules:
  0.0 148.2 jit_solution(1750779593780236209)
XLA Ops:
  0.6 1.6 %collective-permute-start = (f32[128,256]{1,0:T(8,128)}, f32[128,256]{1,0:T(8,128)S(1)}, u32[]{:S(2)}, u32[]{:S(2)}) collective-permute-start(f32[128,256]{1,0:T(8,128)} %param.4), channel_id=1, source_target_pairs={{0,0},{1,1},{2,2},{3,3},{4,4},{5,5},{6,6},{7,7},{8,128},{9,129},{1... | collective-permute-start | bytes 393224 | tf_op jit(solution)/shard_map/ppermute | solution.py:46
  2.2 8.7 %all-gather = f32[512,128]{1,0:T(8,128)S(1)} all-gather(f32[256,128]{1,0:T(8,128)} %param.5), channel_id=2, replica_groups=mesh['x'=4,'zh'=4,'zl'=4,'y'=4,'c'=2] {'c'}, dimensions={0}, use_global_device_ids=true | all-gather | bytes 393216 | tf_op jit(solution)/shard_map/all_gather | solution.py:56
  10.9 0.7 fusion.10
  12.2 1.0 stack.53
  13.2 6.3 %all-to-all-start = ((f32[4,256,256]{2,1,0:T(8,128)}), f32[4,256,256]{2,1,0:T(8,128)S(1)}, u32[]{:S(2)}, u32[]{:S(2)}) async-start(f32[4,256,256]{2,1,0:T(8,128)} %stack.53), calls=%async_computation | async-start | bytes 2097152 | tf_op jit(solution)/shard_map/all_to_all | solution.py:61
  19.5 13.9 %all-gather.1 = f32[512,256]{1,0:T(8,128)S(1)} all-gather(f32[128,256]{1,0:T(8,128)S(1)} %collective-permute-done), channel_id=3, replica_groups=mesh['x'=4,'zh'=4,'zl'=4,'y'=4,'c'=2] {'zl'}, dimensions={0}, use_global_device_ids=true | all-gather | bytes 655360 | tf_op jit(solution)/shard_map/all_gather | solution.py:63
  33.5 1.5 %stack.54 = f32[4,4,128,256]{3,2,1,0:T(8,128)} broadcast(f32[4,128,256]{2,1,0:T(8,128)S(1)} %broadcast_multiply_fusion), dimensions={1,2,3} | broadcast | bytes 2621440 | tf_op jit(solution)/shard_map/stack | solution.py:66
  35.0 4.2 %all-to-all-start.1 = ((f32[4,4,128,256]{3,2,1,0:T(8,128)}), f32[4,4,128,256]{3,2,1,0:T(8,128)S(1)}, u32[]{:S(2)}, u32[]{:S(2)}) async-start(f32[4,4,128,256]{3,2,1,0:T(8,128)} %stack.54), calls=%async_computation.1 | async-start | bytes 4194304 | tf_op jit(solution)/shard_map/all_to_all | solution.py:67
  39.2 31.0 %all-gather.2 = f32[512,256]{1,0:T(8,128)} all-gather(f32[128,256]{1,0:T(8,128)S(1)} %collective-permute-done), channel_id=4, replica_groups=mesh['x'=4,'zh'=4,'zl'=4,'y'=4,'c'=2] {'zh'}, dimensions={0}, use_global_device_ids=true | all-gather | bytes 655360 | tf_op jit(solution)/shard_map/all_gather | solution.py:70
  70.2 0.1 fusion.11
  70.4 3.5 %collective-permute-start.1 = (f32[4,128,256]{2,1,0:T(8,128)}, f32[4,128,256]{2,1,0:T(8,128)S(1)}, u32[]{:S(2)}, u32[]{:S(2)}) collective-permute-start(f32[4,128,256]{2,1,0:T(8,128)} %bitcast.6), channel_id=1, source_target_pairs={{0,128},{128,0},{256,384},{384,256},{1,129},{129,1},{257,385},{385... | collective-permute-start | bytes 1572872 | tf_op jit(solution)/shard_map/ppermute | solution.py:72
  73.9 0.4 fusion.3
  74.3 0.4 convolution_add_fusion.2
  74.7 0.4 convolution_add_fusion.1
  75.1 1.2 convolution_add_fusion
  76.2 6.4 %all-to-all-start.2 = ((f32[4,128,256]{2,1,0:T(8,128)}), f32[4,128,256]{2,1,0:T(8,128)S(1)}, u32[]{:S(2)}, u32[]{:S(2)}) async-start(f32[4,128,256]{2,1,0:T(8,128)} %bitcast.11), calls=%async_computation.2 | async-start | bytes 1048576 | tf_op jit(solution)/shard_map/all_to_all | solution.py:81
  82.7 1.1 bitcast_multiply_fusion.7
  83.9 4.2 %collective-permute-start.4 = (f32[256,256]{1,0:T(8,128)S(1)}, f32[256,256]{1,0:T(8,128)S(1)}, u32[]{:S(2)}, u32[]{:S(2)}) collective-permute-start(f32[256,256]{1,0:T(8,128)S(1)} %pad_maximum_fusion.6), channel_id=1, source_target_pairs={{0,6},{2,0},{4,2},{6,4},{1,7},{3,1},{5,3},{7,5},{8,14},{10,8},{12,... | collective-permute-start | bytes 786440 | tf_op jit(solution)/shard_map/ppermute | solution.py:92
  88.1 2.5 %collective-permute-start.3 = (f32[256,256]{1,0:T(8,128)S(1)}, f32[256,256]{1,0:T(8,128)S(1)}, u32[]{:S(2)}, u32[]{:S(2)}) collective-permute-start(f32[256,256]{1,0:T(8,128)S(1)} %pad_maximum_fusion.5), channel_id=1, source_target_pairs={{0,4},{2,6},{4,0},{6,2},{1,5},{3,7},{5,1},{7,3},{8,12},{10,14},{12... | collective-permute-start | bytes 786440 | tf_op jit(solution)/shard_map/ppermute | solution.py:92
  90.7 2.5 %collective-permute-start.2 = (f32[256,256]{1,0:T(8,128)S(1)}, f32[256,256]{1,0:T(8,128)S(1)}, u32[]{:S(2)}, u32[]{:S(2)}) collective-permute-start(f32[256,256]{1,0:T(8,128)S(1)} %pad_maximum_fusion.4), channel_id=1, source_target_pairs={{0,2},{2,4},{4,6},{6,0},{1,3},{3,5},{5,7},{7,1},{8,10},{10,12},{12... | collective-permute-start | bytes 786440 | tf_op jit(solution)/shard_map/ppermute | solution.py:92
  93.3 3.8 %collective-permute-done.3 = f32[256,256]{1,0:T(8,128)S(1)} collective-permute-done((f32[256,256]{1,0:T(8,128)S(1)}, f32[256,256]{1,0:T(8,128)S(1)}, u32[]{:S(2)}, u32[]{:S(2)}) %collective-permute-start.3) | collective-permute-done | bytes 262176 | tf_op jit(solution)/shard_map/ppermute | solution.py:92
  97.0 2.8 %collective-permute-done.2 = f32[256,256]{1,0:T(8,128)S(1)} collective-permute-done((f32[256,256]{1,0:T(8,128)S(1)}, f32[256,256]{1,0:T(8,128)S(1)}, u32[]{:S(2)}, u32[]{:S(2)}) %collective-permute-start.2) | collective-permute-done | bytes 262176 | tf_op jit(solution)/shard_map/ppermute | solution.py:92
  99.9 0.1 pad_maximum_fusion
  100.1 0.1 pad_maximum_fusion.1
  100.2 14.0 %all_gather.27 = f32[256,256]{1,0:T(8,128)S(1)} all-gather(f32[128,256]{1,0:T(8,128)S(1)} %neg.3), channel_id=1, replica_groups=mesh['x'=4,'zh'=4,'zl'=4,'y'=4,'c'=2] {'c'}, dimensions={0}, use_global_device_ids=true | all-gather | bytes 393216 | tf_op jit(solution)/shard_map/all_gather | solution.py:98
  114.3 0.6 fusion.13
  114.9 20.8 %all_to_all.34 = f32[8,32,1024]{2,1,0:T(8,128)S(1)} all-to-all(f32[8,32,1024]{2,1,0:T(8,128)S(1)} %fusion.13), channel_id=1, replica_groups=mesh['x'=4,'zh'=4,'zl'=4,'y'=4,'c'=2] {'y','c'}, dimensions={0} | all-to-all | bytes 2097152 | tf_op jit(solution)/shard_map/all_to_all | solution.py:103
  135.8 0.7 copy_bitcast_fusion
  136.5 3.4 %all-to-all-start.4 = ((f32[4,16,1024]{2,1,0:T(8,128)}), f32[4,16,1024]{2,1,0:T(8,128)S(1)}, u32[]{:S(2)}, u32[]{:S(2)}) async-start(f32[4,16,1024]{2,1,0:T(8,128)} %copy_bitcast_fusion), calls=%async_computation.4 | async-start | bytes 524288 | tf_op jit(solution)/shard_map/all_to_all | solution.py:106
  139.9 0.7 constant_dynamic-slice_fusion.8
  140.6 6.8 %all-to-all-done.4 = f32[4,16,1024]{2,1,0:T(8,128)S(1)} async-done(((f32[4,16,1024]{2,1,0:T(8,128)}), f32[4,16,1024]{2,1,0:T(8,128)S(1)}, u32[]{:S(2)}, u32[]{:S(2)}) %all-to-all-start.4) | async-done | bytes 262176 | tf_op jit(solution)/shard_map/all_to_all | solution.py:106
  147.5 0.6 sub.15
  (37 shorter events, 1.0 us)
Async XLA Ops:
  0.6 11.6 %collective-permute-start = (f32[128,256]{1,0:T(8,128)}, f32[128,256]{1,0:T(8,128)S(1)}, u32[]{:S(2)}, u32[]{:S(2)}) collective-permute-start(f32[128,256]{1,0:T(8,128)} %param.4), channel_id=1, source_target_pairs={{0,0},{1,1},{2,2},{3,3},{4,4},{5,5},{6,6},{7,7},{8,128},{9,129},{1... | collective-permute-start | bytes 393224 | tf_op jit(solution)/shard_map/ppermute | solution.py:46
  13.2 20.2 %all-to-all-start = ((f32[4,256,256]{2,1,0:T(8,128)}), f32[4,256,256]{2,1,0:T(8,128)S(1)}, u32[]{:S(2)}, u32[]{:S(2)}) async-start(f32[4,256,256]{2,1,0:T(8,128)} %stack.53), calls=%async_computation | async-start | bytes 2097152 | tf_op jit(solution)/shard_map/all_to_all | solution.py:61
  35.0 35.2 %all-to-all-start.1 = ((f32[4,4,128,256]{3,2,1,0:T(8,128)}), f32[4,4,128,256]{3,2,1,0:T(8,128)S(1)}, u32[]{:S(2)}, u32[]{:S(2)}) async-start(f32[4,4,128,256]{3,2,1,0:T(8,128)} %stack.54), calls=%async_computation.1 | async-start | bytes 4194304 | tf_op jit(solution)/shard_map/all_to_all | solution.py:67
  70.4 12.2 %collective-permute-start.1 = (f32[4,128,256]{2,1,0:T(8,128)}, f32[4,128,256]{2,1,0:T(8,128)S(1)}, u32[]{:S(2)}, u32[]{:S(2)}) collective-permute-start(f32[4,128,256]{2,1,0:T(8,128)} %bitcast.6), channel_id=1, source_target_pairs={{0,128},{128,0},{256,384},{384,256},{1,129},{129,1},{257,385},{385... | collective-permute-start | bytes 1572872 | tf_op jit(solution)/shard_map/ppermute | solution.py:72
  76.2 23.9 %all-to-all-start.2 = ((f32[4,128,256]{2,1,0:T(8,128)}), f32[4,128,256]{2,1,0:T(8,128)S(1)}, u32[]{:S(2)}, u32[]{:S(2)}) async-start(f32[4,128,256]{2,1,0:T(8,128)} %bitcast.11), calls=%async_computation.2 | async-start | bytes 1048576 | tf_op jit(solution)/shard_map/all_to_all | solution.py:81
  83.9 9.4 %collective-permute-start.4 = (f32[256,256]{1,0:T(8,128)S(1)}, f32[256,256]{1,0:T(8,128)S(1)}, u32[]{:S(2)}, u32[]{:S(2)}) collective-permute-start(f32[256,256]{1,0:T(8,128)S(1)} %pad_maximum_fusion.6), channel_id=1, source_target_pairs={{0,6},{2,0},{4,2},{6,4},{1,7},{3,1},{5,3},{7,5},{8,14},{10,8},{12,... | collective-permute-start | bytes 786440 | tf_op jit(solution)/shard_map/ppermute | solution.py:92
  88.1 8.9 %collective-permute-start.3 = (f32[256,256]{1,0:T(8,128)S(1)}, f32[256,256]{1,0:T(8,128)S(1)}, u32[]{:S(2)}, u32[]{:S(2)}) collective-permute-start(f32[256,256]{1,0:T(8,128)S(1)} %pad_maximum_fusion.5), channel_id=1, source_target_pairs={{0,4},{2,6},{4,0},{6,2},{1,5},{3,7},{5,1},{7,3},{8,12},{10,14},{12... | collective-permute-start | bytes 786440 | tf_op jit(solution)/shard_map/ppermute | solution.py:92
  90.7 9.2 %collective-permute-start.2 = (f32[256,256]{1,0:T(8,128)S(1)}, f32[256,256]{1,0:T(8,128)S(1)}, u32[]{:S(2)}, u32[]{:S(2)}) collective-permute-start(f32[256,256]{1,0:T(8,128)S(1)} %pad_maximum_fusion.4), channel_id=1, source_target_pairs={{0,2},{2,4},{4,6},{6,0},{1,3},{3,5},{5,7},{7,1},{8,10},{10,12},{12... | collective-permute-start | bytes 786440 | tf_op jit(solution)/shard_map/ppermute | solution.py:92
  135.7 11.8 %copy-start = (f32[8,2048]{1,0:T(8,128)S(1)}, f32[8,2048]{1,0:T(8,128)}, u32[]{:S(2)}) copy-start(f32[8,2048]{1,0:T(8,128)} %param.6) | copy-start | bytes 196612
  136.5 10.9 %all-to-all-start.4 = ((f32[4,16,1024]{2,1,0:T(8,128)}), f32[4,16,1024]{2,1,0:T(8,128)S(1)}, u32[]{:S(2)}, u32[]{:S(2)}) async-start(f32[4,16,1024]{2,1,0:T(8,128)} %copy_bitcast_fusion), calls=%async_computation.4 | async-start | bytes 524288 | tf_op jit(solution)/shard_map/all_to_all | solution.py:106

commit v8 on v6

--- a/solution.py
+++ b/solution.py
@@ -44,25 +44,18 @@
     c = lax.axis_index("c")
 
     moved = lax.ppermute(panel, AXES, turn_pairs())
-
-    def pattern_row(x):
-        row = lax.dynamic_slice_in_dim(pattern, (x * 4 + y) * 2 + c, 1, 0)
-        return row.astype(jnp.float32).reshape(4, 4, 2)
-
-    row, pair_row = pattern_row(x), pattern_row(x ^ 1)
-    mask = jnp.repeat(pick(row, zh, 1), 128, axis=1)[:, None, :]
-    masks = [jnp.repeat(pick(r, zl), 128, axis=1)[:, None, :] for r in (row, pair_row)]
+    own = lax.dynamic_slice(
+        pattern, ((x * 4 + y) * 2 + c, (zl * 4 + zh) * 2), (1, 2)
+    ).astype(jnp.float32)
+    moved = moved * jnp.repeat(own, 128, axis=1)
 
     a_cols = lax.all_gather(ancestor_inverse, "c", axis=0)
     a_cols = jnp.concatenate([a_cols[0], a_cols[1]], axis=1)
-    a_copies, moved, mask, masks = lax.optimization_barrier(
-        (jnp.stack([a_cols] * 4), moved, mask, masks)
-    )
+    a_copies, moved = lax.optimization_barrier((jnp.stack([a_cols] * 4), moved))
     a_all = lax.all_to_all(a_copies, "x", 0, 0, tiled=True).reshape(1024, 256)
 
     over_zl = lax.all_gather(moved, "zl", axis=0)
     over_zl, a_all = lax.optimization_barrier((over_zl, a_all))
-    over_zl = over_zl * mask
     copies = lax.optimization_barrier(jnp.stack([over_zl] * 4))
     by_y = lax.all_to_all(copies, "y", 0, 0, tiled=True)
 
@@ -82,10 +75,7 @@
     summed = -jnp.sum(summed.reshape(4, 128, 256), axis=0)
 
     def column(index):
-        pair = (over_zh, pair_zh)
-        return jnp.concatenate(
-            [pick(b, index) * pick(m, index) for b, m in zip(pair, masks)]
-        )
+        return jnp.concatenate([pick(over_zh, index), pick(pair_zh, index)])
 
     over_zh, pair_zh, _ = lax.optimization_barrier((over_zh, pair_zh, partial))
     pieces = [column(y)] + [

time: 150 us -> 150 us (level)
  transfers between devices with their start and end apart: 9 -> 9, of which waited for: 3 -> 4; matrix products, arithmetic and copies ran while one was open for 4% -> 4% of each run, Pallas kernels for 0% -> 0%
where the time goes in v8:
time: 150 us; the launch traced here: 148 us
  blocking collectives  88.2 us (59%)
  starting transfers between devices  34.9 us (23%)
  waiting for transfers between devices  13.6 us (9%)
  local copies, waits for them, and re-layouts  5.55 us (4%)
  matrix products  2.93 us (2%)
  other arithmetic  1.86 us (1%)
    all_gather x1, blocking collectives, on_device(): over_zh = lax.all_gather(moved, 'zh', axis=0)  31 us
    all_to_all x1, blocking collectives, on_device(): over_y = lax.all_to_all(coupling, ('y', 'c'), 0, 0, tiled=True)  21.4 us
    all_gather x1, blocking collectives, on_device(): over_zl = lax.all_gather(moved, 'zl', axis=0)  13.9 us
    all_gather x1, blocking collectives, on_device(): rows = lax.all_gather(summed, 'c', axis=0, tiled=True)  13.2 us
    ppermute x3, starting transfers between devices, on_device(): lax.ppermute(column((y + s) % 4), 'y', shift_pairs(s))  9.19 us
    all_gather x1, blocking collectives, on_device(): a_cols = lax.all_gather(ancestor_inverse, 'c', axis=0)  8.71 us
    all_to_all x1, waiting for transfers between devices, on_device(): over_l = lax.all_to_all(sum_y, 'zl', 0, 0, tiled=True)  6.84 us
    all_to_all x1, starting transfers between devices, on_device(): a_all = lax.all_to_all(a_copies, 'x', 0, 0, tiled=True).reshape(1024, 256)  6.7 us
  transfers between devices with their start and end apart: 9, of which 4 were waited for; matrix products, arithmetic and copies ran while one was open for 4% of the time, Pallas kernels for 0%

profile of v8, /device:TPU:1, one launch (start us, length us, event | category | flops | bytes accessed | tf_op | source)
XLA Modules:
  0.0 148.1 jit_solution(2182988819789580957)
XLA Ops:
  0.6 1.6 %collective-permute-start = (f32[128,256]{1,0:T(8,128)}, f32[128,256]{1,0:T(8,128)S(1)}, u32[]{:S(2)}, u32[]{:S(2)}) collective-permute-start(f32[128,256]{1,0:T(8,128)} %param.4), channel_id=1, source_target_pairs={{0,0},{1,1},{2,2},{3,3},{4,4},{5,5},{6,6},{7,7},{8,128},{9,129},{1... | collective-permute-start | bytes 393224 | tf_op jit(solution)/shard_map/ppermute | solution.py:46
  2.2 8.7 %all-gather = f32[512,128]{1,0:T(8,128)S(1)} all-gather(f32[256,128]{1,0:T(8,128)} %param.5), channel_id=2, replica_groups=mesh['x'=4,'zh'=4,'zl'=4,'y'=4,'c'=2] {'c'}, dimensions={0}, use_global_device_ids=true | all-gather | bytes 393216 | tf_op jit(solution)/shard_map/all_gather | solution.py:52
  10.9 0.8 convert_bitcast_fusion
  11.8 1.1 stack.53
  12.9 6.7 %all-to-all-start = ((f32[4,256,256]{2,1,0:T(8,128)}), f32[4,256,256]{2,1,0:T(8,128)S(1)}, u32[]{:S(2)}, u32[]{:S(2)}) async-start(f32[4,256,256]{2,1,0:T(8,128)} %stack.53), calls=%async_computation | async-start | bytes 2097152 | tf_op jit(solution)/shard_map/all_to_all | solution.py:55
  19.6 13.9 %all-gather.1 = f32[512,256]{1,0:T(8,128)S(1)} all-gather(f32[128,256]{1,0:T(8,128)S(1)} %broadcast_multiply_fusion), channel_id=3, replica_groups=mesh['x'=4,'zh'=4,'zl'=4,'y'=4,'c'=2] {'zl'}, dimensions={0}, use_global_device_ids=true | all-gather | bytes 655360 | tf_op jit(solution)/shard_map/all_gather | solution.py:57
  33.5 1.5 %stack.54 = f32[4,4,128,256]{3,2,1,0:T(8,128)} broadcast(f32[4,128,256]{2,1,0:T(8,128)S(1)} %bitcast.77), dimensions={1,2,3} | broadcast | bytes 2621440 | tf_op jit(solution)/shard_map/stack | solution.py:59
  35.0 4.2 %all-to-all-start.1 = ((f32[4,4,128,256]{3,2,1,0:T(8,128)}), f32[4,4,128,256]{3,2,1,0:T(8,128)S(1)}, u32[]{:S(2)}, u32[]{:S(2)}) async-start(f32[4,4,128,256]{3,2,1,0:T(8,128)} %stack.54), calls=%async_computation.1 | async-start | bytes 4194304 | tf_op jit(solution)/shard_map/all_to_all | solution.py:60
  39.2 31.0 %all-gather.2 = f32[512,256]{1,0:T(8,128)} all-gather(f32[128,256]{1,0:T(8,128)S(1)} %broadcast_multiply_fusion), channel_id=4, replica_groups=mesh['x'=4,'zh'=4,'zl'=4,'y'=4,'c'=2] {'zh'}, dimensions={0}, use_global_device_ids=true | all-gather | bytes 655360 | tf_op jit(solution)/shard_map/all_gather | solution.py:63
  70.2 0.1 fusion.5
  70.3 3.5 %collective-permute-start.1 = (f32[4,128,256]{2,1,0:T(8,128)}, f32[4,128,256]{2,1,0:T(8,128)S(1)}, u32[]{:S(2)}, u32[]{:S(2)}) collective-permute-start(f32[4,128,256]{2,1,0:T(8,128)} %bitcast.4), channel_id=1, source_target_pairs={{0,128},{128,0},{256,384},{384,256},{1,129},{129,1},{257,385},{385... | collective-permute-start | bytes 1572872 | tf_op jit(solution)/shard_map/ppermute | solution.py:65
  73.8 0.4 fusion.3
  74.2 0.4 convolution_add_fusion.2
  74.6 0.4 convolution_add_fusion.1
  75.0 1.2 convolution_add_fusion
  76.2 6.4 %all-to-all-start.2 = ((f32[4,128,256]{2,1,0:T(8,128)}), f32[4,128,256]{2,1,0:T(8,128)S(1)}, u32[]{:S(2)}, u32[]{:S(2)}) async-start(f32[4,128,256]{2,1,0:T(8,128)} %bitcast.9), calls=%async_computation.2 | async-start | bytes 1048576 | tf_op jit(solution)/shard_map/all_to_all | solution.py:74
  82.6 1.2 dynamic-slice_bitcast_fusion.10
  83.8 4.2 %collective-permute-start.4 = (f32[256,256]{1,0:T(8,128)S(1)}, f32[256,256]{1,0:T(8,128)S(1)}, u32[]{:S(2)}, u32[]{:S(2)}) collective-permute-start(f32[256,256]{1,0:T(8,128)S(1)} %pad_maximum_fusion.6), channel_id=1, source_target_pairs={{0,6},{2,0},{4,2},{6,4},{1,7},{3,1},{5,3},{7,5},{8,14},{10,8},{12,... | collective-permute-start | bytes 786440 | tf_op jit(solution)/shard_map/ppermute | solution.py:82
  88.0 2.5 %collective-permute-start.3 = (f32[256,256]{1,0:T(8,128)S(1)}, f32[256,256]{1,0:T(8,128)S(1)}, u32[]{:S(2)}, u32[]{:S(2)}) collective-permute-start(f32[256,256]{1,0:T(8,128)S(1)} %pad_maximum_fusion.5), channel_id=1, source_target_pairs={{0,4},{2,6},{4,0},{6,2},{1,5},{3,7},{5,1},{7,3},{8,12},{10,14},{12... | collective-permute-start | bytes 786440 | tf_op jit(solution)/shard_map/ppermute | solution.py:82
  90.6 2.5 %collective-permute-start.2 = (f32[256,256]{1,0:T(8,128)S(1)}, f32[256,256]{1,0:T(8,128)S(1)}, u32[]{:S(2)}, u32[]{:S(2)}) collective-permute-start(f32[256,256]{1,0:T(8,128)S(1)} %pad_maximum_fusion.4), channel_id=1, source_target_pairs={{0,2},{2,4},{4,6},{6,0},{1,3},{3,5},{5,7},{7,1},{8,10},{10,12},{12... | collective-permute-start | bytes 786440 | tf_op jit(solution)/shard_map/ppermute | solution.py:82
  93.2 3.8 %collective-permute-done.3 = f32[256,256]{1,0:T(8,128)S(1)} collective-permute-done((f32[256,256]{1,0:T(8,128)S(1)}, f32[256,256]{1,0:T(8,128)S(1)}, u32[]{:S(2)}, u32[]{:S(2)}) %collective-permute-start.3) | collective-permute-done | bytes 262176 | tf_op jit(solution)/shard_map/ppermute | solution.py:82
  97.0 2.8 %collective-permute-done.2 = f32[256,256]{1,0:T(8,128)S(1)} collective-permute-done((f32[256,256]{1,0:T(8,128)S(1)}, f32[256,256]{1,0:T(8,128)S(1)}, u32[]{:S(2)}, u32[]{:S(2)}) %collective-permute-start.2) | collective-permute-done | bytes 262176 | tf_op jit(solution)/shard_map/ppermute | solution.py:82
  100.0 0.1 pad_maximum_fusion.1
  100.1 0.1 all-to-all-done.2
  100.3 13.2 %all_gather.27 = f32[256,256]{1,0:T(8,128)S(1)} all-gather(f32[128,256]{1,0:T(8,128)S(1)} %neg.3), channel_id=1, replica_groups=mesh['x'=4,'zh'=4,'zl'=4,'y'=4,'c'=2] {'c'}, dimensions={0}, use_global_device_ids=true | all-gather | bytes 393216 | tf_op jit(solution)/shard_map/all_gather | solution.py:88
  113.5 0.6 fusion.7
  114.2 21.4 %all_to_all.34 = f32[8,32,1024]{2,1,0:T(8,128)S(1)} all-to-all(f32[8,32,1024]{2,1,0:T(8,128)S(1)} %fusion.7), channel_id=1, replica_groups=mesh['x'=4,'zh'=4,'zl'=4,'y'=4,'c'=2] {'y','c'}, dimensions={0} | all-to-all | bytes 2097152 | tf_op jit(solution)/shard_map/all_to_all | solution.py:93
  135.7 0.7 copy_bitcast_fusion
  136.4 3.4 %all-to-all-start.4 = ((f32[4,16,1024]{2,1,0:T(8,128)}), f32[4,16,1024]{2,1,0:T(8,128)S(1)}, u32[]{:S(2)}, u32[]{:S(2)}) async-start(f32[4,16,1024]{2,1,0:T(8,128)} %copy_bitcast_fusion), calls=%async_computation.4 | async-start | bytes 524288 | tf_op jit(solution)/shard_map/all_to_all | solution.py:96
  139.8 0.7 constant_dynamic-slice_fusion
  140.5 6.8 %all-to-all-done.4 = f32[4,16,1024]{2,1,0:T(8,128)S(1)} async-done(((f32[4,16,1024]{2,1,0:T(8,128)}), f32[4,16,1024]{2,1,0:T(8,128)S(1)}, u32[]{:S(2)}, u32[]{:S(2)}) %all-to-all-start.4) | async-done | bytes 262176 | tf_op jit(solution)/shard_map/all_to_all | solution.py:96
  147.4 0.6 sub.15
  (25 shorter events, 0.6 us)
Async XLA Ops:
  0.6 11.2 %collective-permute-start = (f32[128,256]{1,0:T(8,128)}, f32[128,256]{1,0:T(8,128)S(1)}, u32[]{:S(2)}, u32[]{:S(2)}) collective-permute-start(f32[128,256]{1,0:T(8,128)} %param.4), channel_id=1, source_target_pairs={{0,0},{1,1},{2,2},{3,3},{4,4},{5,5},{6,6},{7,7},{8,128},{9,129},{1... | collective-permute-start | bytes 393224 | tf_op jit(solution)/shard_map/ppermute | solution.py:46
  12.9 20.6 %all-to-all-start = ((f32[4,256,256]{2,1,0:T(8,128)}), f32[4,256,256]{2,1,0:T(8,128)S(1)}, u32[]{:S(2)}, u32[]{:S(2)}) async-start(f32[4,256,256]{2,1,0:T(8,128)} %stack.53), calls=%async_computation | async-start | bytes 2097152 | tf_op jit(solution)/shard_map/all_to_all | solution.py:55
  35.0 35.2 %all-to-all-start.1 = ((f32[4,4,128,256]{3,2,1,0:T(8,128)}), f32[4,4,128,256]{3,2,1,0:T(8,128)S(1)}, u32[]{:S(2)}, u32[]{:S(2)}) async-start(f32[4,4,128,256]{3,2,1,0:T(8,128)} %stack.54), calls=%async_computation.1 | async-start | bytes 4194304 | tf_op jit(solution)/shard_map/all_to_all | solution.py:60
  70.3 12.2 %collective-permute-start.1 = (f32[4,128,256]{2,1,0:T(8,128)}, f32[4,128,256]{2,1,0:T(8,128)S(1)}, u32[]{:S(2)}, u32[]{:S(2)}) collective-permute-start(f32[4,128,256]{2,1,0:T(8,128)} %bitcast.4), channel_id=1, source_target_pairs={{0,128},{128,0},{256,384},{384,256},{1,129},{129,1},{257,385},{385... | collective-permute-start | bytes 1572872 | tf_op jit(solution)/shard_map/ppermute | solution.py:65
  76.2 24.0 %all-to-all-start.2 = ((f32[4,128,256]{2,1,0:T(8,128)}), f32[4,128,256]{2,1,0:T(8,128)S(1)}, u32[]{:S(2)}, u32[]{:S(2)}) async-start(f32[4,128,256]{2,1,0:T(8,128)} %bitcast.9), calls=%async_computation.2 | async-start | bytes 1048576 | tf_op jit(solution)/shard_map/all_to_all | solution.py:74
  83.8 9.4 %collective-permute-start.4 = (f32[256,256]{1,0:T(8,128)S(1)}, f32[256,256]{1,0:T(8,128)S(1)}, u32[]{:S(2)}, u32[]{:S(2)}) collective-permute-start(f32[256,256]{1,0:T(8,128)S(1)} %pad_maximum_fusion.6), channel_id=1, source_target_pairs={{0,6},{2,0},{4,2},{6,4},{1,7},{3,1},{5,3},{7,5},{8,14},{10,8},{12,... | collective-permute-start | bytes 786440 | tf_op jit(solution)/shard_map/ppermute | solution.py:82
  88.0 8.9 %collective-permute-start.3 = (f32[256,256]{1,0:T(8,128)S(1)}, f32[256,256]{1,0:T(8,128)S(1)}, u32[]{:S(2)}, u32[]{:S(2)}) collective-permute-start(f32[256,256]{1,0:T(8,128)S(1)} %pad_maximum_fusion.5), channel_id=1, source_target_pairs={{0,4},{2,6},{4,0},{6,2},{1,5},{3,7},{5,1},{7,3},{8,12},{10,14},{12... | collective-permute-start | bytes 786440 | tf_op jit(solution)/shard_map/ppermute | solution.py:82
  90.6 9.2 %collective-permute-start.2 = (f32[256,256]{1,0:T(8,128)S(1)}, f32[256,256]{1,0:T(8,128)S(1)}, u32[]{:S(2)}, u32[]{:S(2)}) collective-permute-start(f32[256,256]{1,0:T(8,128)S(1)} %pad_maximum_fusion.4), channel_id=1, source_target_pairs={{0,2},{2,4},{4,6},{6,0},{1,3},{3,5},{5,7},{7,1},{8,10},{10,12},{12... | collective-permute-start | bytes 786440 | tf_op jit(solution)/shard_map/ppermute | solution.py:82
  135.6 11.8 %copy-start = (f32[8,2048]{1,0:T(8,128)S(1)}, f32[8,2048]{1,0:T(8,128)}, u32[]{:S(2)}) copy-start(f32[8,2048]{1,0:T(8,128)} %param.6) | copy-start | bytes 196612
  136.4 10.9 %all-to-all-start.4 = ((f32[4,16,1024]{2,1,0:T(8,128)}), f32[4,16,1024]{2,1,0:T(8,128)S(1)}, u32[]{:S(2)}, u32[]{:S(2)}) async-start(f32[4,16,1024]{2,1,0:T(8,128)} %copy_bitcast_fusion), calls=%async_computation.4 | async-start | bytes 524288 | tf_op jit(solution)/shard_map/all_to_all | solution.py:96
